TPU v7x, 256 devices: a whole 4x4x8 slice. The times are simulated.
256 devices in a mesh: lon: 16 (over z, y_lo), lat: 16 (over y_hi, x, core).
Axes of the slice: x: 4, y: 4 (y_hi: 2, y_lo: 2; y = y_hi * 2 + y_lo), z: 8, core: 2. Of those that a mesh axis runs over, the one named last changes fastest.
Arguments:
- tracers: float32 [2, 4, 256, 2048], P(None, None, 'lat', 'lon'), may hold values from -6 to 6
- land_mask: int32 [256, 2048], P('lat', 'lon'), may hold values 0 or 1
- level_counts: int32 [256, 2048], P('lat', 'lon'), may hold values from 1 to 4
- fold_partner: int32 [2048], P('lon'), may hold values from 0 to 2047, as said below
- cotangent: float32 [2, 4, 256, 2048], P(None, None, 'lat', 'lon'), may hold values from -6 to 6
- w_first: float32 [6, 128], replicated, may hold values from -2.5 to 2.5
- b_first: float32 [128], replicated, may hold values from -3 to 3
- w_second: float32 [128, 128], replicated, may hold values from -0.5 to 0.5
- b_second: float32 [128], replicated, may hold values from -3 to 3
- w_head: float32 [128], replicated, may hold values from -0.5 to 0.5
- b_head: float32 [1], replicated, may hold values from -3 to 3
Outputs:
- tracers_out: float32 [2, 4, 256, 2048], P(None, None, 'lat', 'lon')
- tracer_grad: float32 [2, 4, 256, 2048], P(None, None, 'lat', 'lon')
- w_first_grad: float32 [6, 128], replicated
- w_second_grad: float32 [128, 128], replicated
- w_head_grad: float32 [128], replicated
Inputs may be any that keep to these rules, and one draw needn't show every extreme that they name: fold_partner[x] = (s - x) mod 2048 for one odd whole number s of the draw: the mirror about the fold line, so fold_partner[fold_partner[x]] = x and fold_partner[x] != x.
All inputs are finite; a program needn't handle non-finite values. No bound on the sum of `land_mask` on one device may be relied on, other than what follows from the above.
Results may differ from a plain program's by a relative error of at most 0.0003.
Values sent between devices are 32-bit elements; how exact they have to be, the bound alone decides.
A program may use at most 128 MiB of HBM per device.

v0:
```python
import math

import jax
import jax.numpy as jnp
from jax import lax
from jax.sharding import PartitionSpec as P

STEPS = 2


KMAX = 0.24
HIGH = lax.Precision.HIGHEST


def padded(cells, sides, width, closed):
    for axis, dim in sides:
        count = lax.axis_size(axis)
        ends = count if closed else count - 1
        head = lax.slice_in_dim(cells, 0, width, axis=dim)
        tail = lax.slice_in_dim(cells, cells.shape[dim] - width, cells.shape[dim], axis=dim)
        cells = jnp.concatenate(
            [
                lax.ppermute(tail, axis, [(i, (i + 1) % count) for i in range(ends)]),
                cells,
                lax.ppermute(head, axis, [((i + 1) % count, i) for i in range(ends)]),
            ],
            axis=dim,
        )
    return cells


def features(tracer, wet_cells):
    rest = [(0, 0)] * (tracer.ndim - 2)
    vertical = (tracer[:, 1:] - tracer[:, :-1]) * (wet_cells[1:] * wet_cells[:-1])
    upward = jnp.pad(-vertical, [(0, 0), (1, 0)] + rest)
    downward = jnp.pad(vertical, [(0, 0), (0, 1)] + rest)
    return jnp.concatenate([tracer, upward, downward], 0)


def closure(flat, w_first, b_first, w_second, b_second, w_head, b_head):
    first = jnp.tanh(jnp.dot(w_first.T, flat, precision=HIGH) + b_first[:, None])
    second = jnp.tanh(jnp.dot(w_second.T, first, precision=HIGH) + b_second[:, None])
    return jnp.dot(w_head, second, precision=HIGH) + b_head[0]


def kappa_of(tracer, wet_cells, weights):
    feats = features(tracer, wet_cells)
    flat = feats.reshape(feats.shape[0], -1)
    output = closure(flat, *weights).reshape(wet_cells.shape)
    return KMAX * jax.nn.sigmoid(output) * wet_cells


def beside_all(core, west_col, east_col, south_row, north_row):
    east = jnp.concatenate([core[..., 1:], east_col[..., None]], -1)
    west = jnp.concatenate([west_col[..., None], core[..., :-1]], -1)
    north = jnp.concatenate([core[..., 1:, :], north_row[..., None, :]], -2)
    south = jnp.concatenate([south_row[..., None, :], core[..., :-1, :]], -2)
    return [east, west, north, south]


def per_device(
    tracers,
    land_mask,
    level_counts,
    fold_partner,
    cotangent,
    w_first,
    b_first,
    w_second,
    b_second,
    w_head,
    b_head,
):
    depth = tracers.shape[1]
    rows_here = tracers.shape[2]
    cols_here = tracers.shape[3]
    below = (jnp.arange(depth, dtype=jnp.int32)[:, None, None] < level_counts[None]).astype(
        jnp.float32
    )
    wet_cells = land_mask[None].astype(jnp.float32) * below
    at_top = lax.axis_index("lat") == lax.axis_size("lat") - 1
    weights = (w_first, b_first, w_second, b_second, w_head, b_head)
    saved = []
    current = tracers
    for number in range(STEPS):
        kappa = kappa_of(current, wet_cells, weights)
        payload = jnp.concatenate([current, kappa[None], wet_cells[None]], 0)
        lon_ext = padded(payload, (("lon", 3),), 1, True)
        lat_ext = padded(payload, (("lat", 2),), 1, False)
        top_rows = lax.all_gather(payload[:, :, -1, :], "lon", axis=2, tiled=True)
        fold_row = jnp.take(top_rows, fold_partner, axis=2)
        north_row = jnp.where(at_top, fold_row, lat_ext[:, :, -1, :])
        sides = beside_all(
            payload, lon_ext[..., 0], lon_ext[..., -1], lat_ext[:, :, 0, :], north_row
        )
        change = jnp.zeros_like(current)
        coefficients = []
        pair_masks = []
        contrasts = []
        for side in sides:
            coefficient = 0.5 * (kappa + side[2]) * wet_cells * side[3]
            contrast = side[:2] - current
            change = change + coefficient * contrast
            coefficients.append(coefficient)
            pair_masks.append(0.5 * wet_cells * side[3])
            contrasts.append(contrast)
        saved.append((current, coefficients, pair_masks, contrasts))
        current = current + change

    def kappa_by(tracer, first, second, head_row):
        return kappa_of(tracer, wet_cells, (first, b_first, second, b_second, head_row, b_head))

    adjoint = cotangent
    totals = (jnp.zeros_like(w_first), jnp.zeros_like(w_second), jnp.zeros_like(w_head))
    for number in reversed(range(STEPS)):
        state, coefficients, pair_masks, contrasts = saved[number]
        lon_ext = padded(adjoint, (("lon", 3),), 1, True)
        lat_ext = padded(adjoint, (("lat", 2),), 1, False)
        top_rows = lax.all_gather(adjoint[:, :, -1, :], "lon", axis=2, tiled=True)
        fold_row = jnp.take(top_rows, fold_partner, axis=2)
        north_row = jnp.where(at_top, fold_row, lat_ext[:, :, -1, :])
        sides = beside_all(
            adjoint, lon_ext[..., 0], lon_ext[..., -1], lat_ext[:, :, 0, :], north_row
        )
        direct = adjoint
        kappa_bar = jnp.zeros_like(wet_cells)
        for side, coefficient, pair_mask, contrast in zip(
            sides, coefficients, pair_masks, contrasts
        ):
            direct = direct + coefficient * (side - adjoint)
            kappa_bar = kappa_bar + pair_mask * jnp.sum(contrast * (adjoint - side), 0)
        unused, pullback = jax.vjp(kappa_by, state, w_first, w_second, w_head)
        tracer_bar, grad_first, grad_second, grad_head = pullback(kappa_bar)
        adjoint = direct + tracer_bar
        local_sums = (grad_first, grad_second, grad_head)
        totals = tuple((left + right for left, right in zip(totals, local_sums)))
    totals = lax.psum(totals, ("lon", "lat"))
    cells_all = lax.axis_size("lon") * cols_here * lax.axis_size("lat") * rows_here * depth
    scale = 1.0 / math.sqrt(cells_all)
    return (current, adjoint, totals[0] * scale, totals[1] * scale, totals[2] * scale)


def solution(mesh):
    return jax.shard_map(
        per_device,
        mesh=mesh,
        in_specs=(
            P(None, None, "lat", "lon"),
            P("lat", "lon"),
            P("lat", "lon"),
            P("lon"),
            P(None, None, "lat", "lon"),
            P(),
            P(),
            P(),
            P(),
            P(),
            P(),
        ),
        out_specs=(P(None, None, "lat", "lon"), P(None, None, "lat", "lon"), P(), P(), P()),
        check_vma=False,
    )
```

profile of v0, /device:TPU:1, one launch (start us, length us, event | category | flops | bytes accessed | tf_op | source)
XLA Modules:
  0.0 559.4 jit_solution(5601541821782191995)
XLA Ops:
  12.6 7.4 %fusion.5 = f32[8192,128]{1,0:T(8,128)S(1)} fusion(f32[6,128]{1,0:T(8,128)} %param.20, f32[128]{0:T(128)} %param.21, f32[1,6,64,128]{3,2,1,0:T(8,128)S(1)} %bitcast.171), kind=kOutput, calls=%fused_computation.15 | convolution fusion | flops 76546048 | bytes 4394496 | tf_op jit(solution)/shard_map/dot_general | solution.py:41
  25.7 3.9 fusion.94
  30.3 5.1 collective-permute-start.2
  36.2 4.9 collective-permute-start
  48.6 27.1 %all-gather = f32[4,4,1,2048]{3,1,2,0:T(4,128)S(1)} all-gather(f32[4,4,1,128]{3,1,2,0:T(4,128)} %bitcast.7), channel_id=2, replica_groups=mesh['lon'=16,'lat'=16] {'lon'}, dimensions={3}, use_global_device_ids=true | all-gather | bytes 139264 | tf_op jit(solution)/shard_map/all_gather | solution.py:90
  75.8 23.5 %all-gather.2 = f32[2,4,1,2048]{3,1,2,0:T(4,128)S(1)} all-gather(f32[2,4,1,128]{3,1,2,0:T(4,128)} %bitcast.28), channel_id=4, replica_groups=mesh['lon'=16,'lat'=16] {'lon'}, dimensions={3}, use_global_device_ids=true | all-gather | bytes 69632 | tf_op jit(solution)/shard_map/all_gather | solution.py:119
  109.5 16.9 %collective-permute-start.10 = (f32[2,4,1,128]{3,1,0,2:T(4,128)}, f32[2,4,1,128]{3,1,0,2:T(4,128)S(1)}, u32[]{:S(2)}, u32[]{:S(2)}) collective-permute-start(f32[2,4,1,128]{3,1,0,2:T(4,128)} %bitcast.64), channel_id=1, source_target_pairs={{1,0},{2,1},{3,2},{4,3},{5,4},{6,5},{7,6},{8,7},{9,8},{10,9},{11,1... | collective-permute-start | bytes 12296 | tf_op jit(solution)/shard_map/ppermute | solution.py:25
  135.8 7.4 %fusion.2 = f32[8192,128]{1,0:T(8,128)S(1)} fusion(f32[6,128]{1,0:T(8,128)} %param.20, f32[128]{0:T(128)} %param.21, f32[1,6,64,128]{3,2,1,0:T(8,128)S(1)} %bitcast.173), kind=kOutput, calls=%fused_computation.10 | convolution fusion | flops 76546048 | bytes 4394496 | tf_op jit(solution)/shard_map/dot_general | solution.py:41
  148.8 15.1 %fusion.92 = f32[1,8192]{1,0:T(1,128)S(1)} fusion(f32[128,8192]{0,1:T(8,128)S(1)} %fusion.1, f32[128]{0:T(128)S(1)} %copy-done.27), kind=kOutput, calls=%fused_computation.209 | convolution fusion | flops 12582912 | bytes 4227584 | tf_op jit(solution)/shard_map/dot_general | solution.py:43
  164.3 3.6 collective-permute-start.4
  171.3 23.2 %all-gather.1 = f32[4,4,1,2048]{3,1,2,0:T(4,128)S(1)} all-gather(f32[4,4,1,128]{3,1,2,0:T(4,128)S(1)} %bitcast.223), channel_id=3, replica_groups=mesh['lon'=16,'lat'=16] {'lon'}, dimensions={3}, use_global_device_ids=true | all-gather | bytes 139264 | tf_op jit(solution)/shard_map/all_gather | solution.py:90
  203.6 4.4 collective-permute-done.5
  208.0 9.4 %collective-permute-start.6 = (f32[4,4,1,128]{3,2,1,0:T(1,128)S(1)}, f32[4,4,1,128]{3,2,1,0:T(1,128)S(1)}, u32[]{:S(2)}, u32[]{:S(2)}) collective-permute-start(f32[4,4,1,128]{3,2,1,0:T(1,128)S(1)} %get-tuple-element.92), channel_id=1, source_target_pairs={{1,0},{2,1},{3,2},{4,3},{5,4},{6,5},{7,6},{8,7},{9,8},{10,9},{11,1... | collective-permute-start | bytes 24584 | tf_op jit(solution)/shard_map/ppermute | solution.py:25
  220.5 11.5 %fusion.6 = f32[128,128]{1,0:T(8,128)S(1)} fusion(f32[8192,128]{1,0:T(8,128)} %copy-done.8, f32[128,8192]{0,1:T(8,128)} %copy-done.4, f32[128]{0:T(128)S(1)} %copy-done.27, f32[8192]{0:T(1024)S(1)} %fusion.46), kind=kOutput, calls=%fused_computation.20 | convolution fusion | flops 1615855616 | bytes 8487424 | tf_op jit(solution)/shard_map/transpose(jvp())/dot_general | solution.py:42
  232.0 4.5 convolution_multiply_fusion.1
  236.5 3.6 convolution_bitcast_fusion.1
  250.6 4.2 collective-permute-start.15
  258.2 25.3 %all-gather.3 = f32[2,4,1,2048]{3,1,2,0:T(4,128)S(1)} all-gather(f32[2,4,1,128]{3,1,2,0:T(4,128)} %bitcast.44), channel_id=5, replica_groups=mesh['lon'=16,'lat'=16] {'lon'}, dimensions={3}, use_global_device_ids=true | all-gather | bytes 69632 | tf_op jit(solution)/shard_map/all_gather | solution.py:119
  291.4 7.9 %convolution_multiply_fusion = f32[8192,128]{1,0:T(8,128)} fusion(f32[128,128]{1,0:T(8,128)S(1)} %copy-done, f32[8192,128]{1,0:T(8,128)} %copy-done.6, f32[128,8192]{0,1:T(8,128)} %copy-done.1, f32[8192]{0:T(1024)S(1)} %fusion.47, f32[128]{0:T(128)S(1)} %copy-done.28), kind=kOutput, calls=%fused_computation.4 | convolution fusion | flops 1620049920 | bytes 12681728 | tf_op jit(solution)/shard_map/transpose(jvp())/dot_general | solution.py:42
  299.3 8.7 %fusion.20 = f32[128,128]{1,0:T(8,128)} fusion(f32[128,128]{1,0:T(8,128)S(1)} %fusion.6, f32[8192,128]{1,0:T(8,128)S(1)} %copy-done.7, f32[128,8192]{0,1:T(8,128)S(1)} %copy-done.2, f32[8192]{0:T(1024)S(1)} %fusion.47, f32[128]{0:T(128)S(1)} %copy-done.28), kind=kOutput, calls=%fused_computation.34 | convolution fusion | flops 1615872000 | bytes 8552960 | tf_op jit(solution)/shard_map/transpose(jvp())/dot_general | solution.py:42
  308.0 5.7 %convolution_bitcast_fusion = f32[6,8192]{1,0:T(8,128)S(1)} fusion(f32[8192,128]{1,0:T(8,128)} %convolution_multiply_fusion, f32[6,128]{1,0:T(8,128)S(1)} %copy-done.25), kind=kOutput, calls=%fused_computation.16 | convolution fusion | flops 75497472 | bytes 4393984 | tf_op jit(solution)/shard_map/transpose(jvp())/dot_general | solution.py:41
  313.8 4.0 convolution_add_fusion.4
  319.9 83.0 %all-reduce.8 = (f32[6,128]{1,0:T(8,128)S(1)}, f32[128]{0:T(128)S(1)}) all-reduce(f32[6,128]{1,0:T(8,128)S(1)} %convolution_add_fusion.4, f32[128]{0:T(128)S(1)} %fusion.21), channel_id=1, replica_groups=mesh['lon'=16,'lat'=16] {'lon','lat'}, use_global_device_ids=true, to_apply=%region_8.11 | all-reduce | flops 896 | bytes 7168 | tf_op jit(solution)/shard_map/psum | solution.py:137
  405.7 145.2 %all-reduce.11.cloned.1.call-done = f32[128,128]{1,0:T(8,128)} async-done(((f32[128,128]{1,0:T(8,128)}), f32[128,128]{1,0:T(8,128)}) %all-reduce.11.cloned.1.call-update) | async-done | bytes 65552 | tf_op jit(solution)/shard_map/psum | solution.py:137
  (201 shorter events, 88.1 us)
Async XLA Ops:
  7.2 543.7 %all-reduce.11.cloned.1.call-start = ((), (), s32[]{:S(2)}) async-start(), calls=%async_computation | async-start | bytes 131072 | tf_op jit(solution)/shard_map/psum | solution.py:137
  30.3 102.3 %collective-permute-start.2 = (f32[4,4,1,128]{3,1,0,2:T(4,128)}, f32[4,4,1,128]{3,1,0,2:T(4,128)}, u32[]{:S(2)}, u32[]{:S(2)}) collective-permute-start(f32[4,4,1,128]{3,1,0,2:T(4,128)} %get-tuple-element.101), channel_id=1, source_target_pairs={{1,0},{2,1},{3,2},{4,3},{5,4},{6,5},{7,6},{8,7},{9,8},{10,9},{11,1... | collective-permute-start | bytes 24584 | tf_op jit(solution)/shard_map/ppermute | solution.py:25
  36.2 73.3 %collective-permute-start = (f32[4,4,16,1]{3,1,0,2:T(4,128)}, f32[4,4,16,1]{3,1,0,2:T(4,128)}, u32[]{:S(2)}, u32[]{:S(2)}) collective-permute-start(f32[4,4,16,1]{3,1,0,2:T(4,128)} %get-tuple-element.98), channel_id=1, source_target_pairs={{16,0},{32,16},{48,32},{64,48},{80,64},{96,80},{112,96},{128,112},... | collective-permute-start | bytes 3080 | tf_op jit(solution)/shard_map/ppermute | solution.py:25
  41.1 86.2 %collective-permute-start.1 = (f32[4,4,16,1]{3,1,0,2:T(4,128)}, f32[4,4,16,1]{3,1,0,2:T(4,128)}, u32[]{:S(2)}, u32[]{:S(2)}) collective-permute-start(f32[4,4,16,1]{3,1,0,2:T(4,128)} %get-tuple-element.99), channel_id=1, source_target_pairs={{0,16},{16,32},{32,48},{48,64},{64,80},{80,96},{96,112},{112,128},... | collective-permute-start | bytes 3080 | tf_op jit(solution)/shard_map/ppermute | solution.py:23
  41.1 90.7 %collective-permute-start.3 = (f32[4,4,1,128]{3,1,0,2:T(4,128)}, f32[4,4,1,128]{3,1,0,2:T(4,128)}, u32[]{:S(2)}, u32[]{:S(2)}) collective-permute-start(f32[4,4,1,128]{3,1,0,2:T(4,128)} %get-tuple-element.100), channel_id=1, source_target_pairs={{0,1},{1,2},{2,3},{3,4},{4,5},{5,6},{6,7},{7,8},{8,9},{9,10},{10,1... | collective-permute-start | bytes 24584 | tf_op jit(solution)/shard_map/ppermute | solution.py:23
  45.0 174.5 %collective-permute-start.11 = (f32[2,4,1,128]{3,2,1,0:T(1,128)}, f32[2,4,1,128]{3,2,1,0:T(1,128)}, u32[]{:S(2)}, u32[]{:S(2)}) collective-permute-start(f32[2,4,1,128]{3,2,1,0:T(1,128)} %get-tuple-element.117), channel_id=1, source_target_pairs={{0,1},{1,2},{2,3},{3,4},{4,5},{5,6},{6,7},{7,8},{8,9},{9,10},{10,1... | collective-permute-start | bytes 12296 | tf_op jit(solution)/shard_map/ppermute | solution.py:23
  75.8 50.7 %copy-start.30 = (s32[1024]{0:T(1024)}, s32[1024]{0:T(1024)S(1)}, u32[]{:S(2)}) copy-start(s32[1024]{0:T(1024)S(1)} %pad_clamp_fusion) | copy-start | bytes 12292
  109.5 21.7 %collective-permute-start.10 = (f32[2,4,1,128]{3,1,0,2:T(4,128)}, f32[2,4,1,128]{3,1,0,2:T(4,128)S(1)}, u32[]{:S(2)}, u32[]{:S(2)}) collective-permute-start(f32[2,4,1,128]{3,1,0,2:T(4,128)} %bitcast.64), channel_id=1, source_target_pairs={{1,0},{2,1},{3,2},{4,3},{5,4},{6,5},{7,6},{8,7},{9,8},{10,9},{11,1... | collective-permute-start | bytes 12296 | tf_op jit(solution)/shard_map/ppermute | solution.py:25
  127.3 92.2 %collective-permute-start.8 = (f32[2,4,16,1]{3,2,1,0:T(8,128)}, f32[2,4,16,1]{3,2,1,0:T(8,128)S(1)}, u32[]{:S(2)}, u32[]{:S(2)}) collective-permute-start(f32[2,4,16,1]{3,2,1,0:T(8,128)} %get-tuple-element.112), channel_id=1, source_target_pairs={{16,0},{32,16},{48,32},{64,48},{80,64},{96,80},{112,96},{128,112},... | collective-permute-start | bytes 1544 | tf_op jit(solution)/shard_map/ppermute | solution.py:25
  131.2 88.4 %collective-permute-start.9 = (f32[2,4,16,1]{3,2,1,0:T(8,128)}, f32[2,4,16,1]{3,2,1,0:T(8,128)S(1)}, u32[]{:S(2)}, u32[]{:S(2)}) collective-permute-start(f32[2,4,16,1]{3,2,1,0:T(8,128)} %get-tuple-element.113), channel_id=1, source_target_pairs={{0,16},{16,32},{32,48},{48,64},{64,80},{80,96},{96,112},{112,128},... | collective-permute-start | bytes 1544 | tf_op jit(solution)/shard_map/ppermute | solution.py:23
  164.0 55.5 %copy-start.33 = (pred[128]{0:T(512)(128)(4,1)S(1)}, pred[128]{0:T(512)(128)(4,1)}, u32[]{:S(2)}) copy-start(pred[128]{0:T(512)(128)(4,1)} %compare_and_fusion) | copy-start | bytes 388
  164.3 37.8 %collective-permute-start.4 = (f32[4,4,16,1]{3,2,1,0:T(8,128)S(1)}, f32[4,4,16,1]{3,2,1,0:T(8,128)S(1)}, u32[]{:S(2)}, u32[]{:S(2)}) collective-permute-start(f32[4,4,16,1]{3,2,1,0:T(8,128)S(1)} %get-tuple-element.87), channel_id=1, source_target_pairs={{16,0},{32,16},{48,32},{64,48},{80,64},{96,80},{112,96},{128,112},... | collective-permute-start | bytes 3080 | tf_op jit(solution)/shard_map/ppermute | solution.py:25
  167.9 51.6 %collective-permute-start.7 = (f32[4,4,1,128]{3,2,1,0:T(1,128)S(1)}, f32[4,4,1,128]{3,2,1,0:T(1,128)S(1)}, u32[]{:S(2)}, u32[]{:S(2)}) collective-permute-start(f32[4,4,1,128]{3,2,1,0:T(1,128)S(1)} %get-tuple-element.93), channel_id=1, source_target_pairs={{0,1},{1,2},{2,3},{3,4},{4,5},{5,6},{6,7},{7,8},{8,9},{9,10},{10,1... | collective-permute-start | bytes 24584 | tf_op jit(solution)/shard_map/ppermute | solution.py:23
  202.1 5.9 %collective-permute-start.5 = (f32[4,4,16,1]{3,2,1,0:T(8,128)S(1)}, f32[4,4,16,1]{3,2,1,0:T(8,128)S(1)}, u32[]{:S(2)}, u32[]{:S(2)}) collective-permute-start(f32[4,4,16,1]{3,2,1,0:T(8,128)S(1)} %get-tuple-element.86), channel_id=1, source_target_pairs={{0,16},{16,32},{32,48},{48,64},{64,80},{80,96},{96,112},{112,128},... | collective-permute-start | bytes 3080 | tf_op jit(solution)/shard_map/ppermute | solution.py:23
  208.0 11.4 %collective-permute-start.6 = (f32[4,4,1,128]{3,2,1,0:T(1,128)S(1)}, f32[4,4,1,128]{3,2,1,0:T(1,128)S(1)}, u32[]{:S(2)}, u32[]{:S(2)}) collective-permute-start(f32[4,4,1,128]{3,2,1,0:T(1,128)S(1)} %get-tuple-element.92), channel_id=1, source_target_pairs={{1,0},{2,1},{3,2},{4,3},{5,4},{6,5},{7,6},{8,7},{9,8},{10,9},{11,1... | collective-permute-start | bytes 24584 | tf_op jit(solution)/shard_map/ppermute | solution.py:25
  245.3 44.2 %copy-start.24 = (f32[4,4,1,128]{3,1,0,2:T(4,128)S(1)}, f32[4,4,1,128]{3,1,0,2:T(4,128)}, u32[]{:S(2)}) copy-start(f32[4,4,1,128]{3,1,0,2:T(4,128)} %copy-done.23) | copy-start | bytes 24580
  245.9 42.9 %collective-permute-start.14 = (f32[2,4,1,128]{3,1,0,2:T(4,128)}, f32[2,4,1,128]{3,1,0,2:T(4,128)}, u32[]{:S(2)}, u32[]{:S(2)}) collective-permute-start(f32[2,4,1,128]{3,1,0,2:T(4,128)} %copy.891), channel_id=1, source_target_pairs={{1,0},{2,1},{3,2},{4,3},{5,4},{6,5},{7,6},{8,7},{9,8},{10,9},{11,1... | collective-permute-start | bytes 12296 | tf_op jit(solution)/shard_map/ppermute | solution.py:25
  248.5 41.0 %collective-permute-start.12 = (f32[2,4,16,1]{3,1,0,2:T(4,128)}, f32[2,4,16,1]{3,1,0,2:T(4,128)S(1)}, u32[]{:S(2)}, u32[]{:S(2)}) collective-permute-start(f32[2,4,16,1]{3,1,0,2:T(4,128)} %copy.895), channel_id=1, source_target_pairs={{16,0},{32,16},{48,32},{64,48},{80,64},{96,80},{112,96},{128,112},... | collective-permute-start | bytes 1544 | tf_op jit(solution)/shard_map/ppermute | solution.py:25
  249.1 40.4 %collective-permute-start.13 = (f32[2,4,16,1]{3,1,0,2:T(4,128)}, f32[2,4,16,1]{3,1,0,2:T(4,128)S(1)}, u32[]{:S(2)}, u32[]{:S(2)}) collective-permute-start(f32[2,4,16,1]{3,1,0,2:T(4,128)} %copy.894), channel_id=1, source_target_pairs={{0,16},{16,32},{32,48},{48,64},{64,80},{80,96},{96,112},{112,128},... | collective-permute-start | bytes 1544 | tf_op jit(solution)/shard_map/ppermute | solution.py:23
  250.6 39.2 %collective-permute-start.15 = (f32[2,4,1,128]{3,2,1,0:T(1,128)}, f32[2,4,1,128]{3,2,1,0:T(1,128)}, u32[]{:S(2)}, u32[]{:S(2)}) collective-permute-start(f32[2,4,1,128]{3,2,1,0:T(1,128)} %get-tuple-element.108), channel_id=1, source_target_pairs={{0,1},{1,2},{2,3},{3,4},{4,5},{5,6},{6,7},{7,8},{8,9},{9,10},{10,1... | collective-permute-start | bytes 12296 | tf_op jit(solution)/shard_map/ppermute | solution.py:23
  313.7 89.9 %copy-start.16 = (f32[4,16,128]{2,0,1:T(4,128)S(1)}, f32[4,16,128]{2,0,1:T(4,128)}, u32[]{:S(2)}) copy-start(f32[4,16,128]{2,0,1:T(4,128)} %copy-done.15) | copy-start | bytes 98308
  313.7 89.9 %copy-start.18 = (f32[4,16,128]{2,0,1:T(4,128)S(1)}, f32[4,16,128]{2,0,1:T(4,128)}, u32[]{:S(2)}) copy-start(f32[4,16,128]{2,0,1:T(4,128)} %copy-done.17) | copy-start | bytes 98308
  313.8 89.9 %copy-start.20 = (f32[4,16,128]{2,0,1:T(4,128)S(1)}, f32[4,16,128]{2,0,1:T(4,128)}, u32[]{:S(2)}) copy-start(f32[4,16,128]{2,0,1:T(4,128)} %copy-done.19) | copy-start | bytes 98308
  313.8 90.0 %copy-start.14 = (f32[4,16,128]{2,1,0:T(8,128)S(1)}, f32[4,16,128]{2,1,0:T(8,128)}, u32[]{:S(2)}) copy-start(f32[4,16,128]{2,1,0:T(8,128)} %copy-done.13) | copy-start | bytes 98308
  (29 other events, 389.1 us)
Sparse Core Ops, SparseCore 0:
  308.1 242.6 all-reduce.10
where the time goes:
time: 570 us; the launch traced here: 559 us
  blocking collectives  182 us (32%)
  waiting for transfers between devices  152 us (27%)
  matrix products  94.5 us (17%)
  starting transfers between devices  59.4 us (10%)
  local copies, waits for them, and re-layouts  35.4 us (6%)
  other arithmetic  20.5 us (4%)
  between operations  15.9 us (3%)
    psum x1, waiting for transfers between devices, per_device(): totals = lax.psum(totals, ('lon', 'lat'))  145 us
    psum x1, blocking collectives, per_device(): totals = lax.psum(totals, ('lon', 'lat'))  83 us
    all_gather x2, blocking collectives, per_device(): top_rows = lax.all_gather(payload[:, :, -1, :], 'lon', axis=2, tiled=True)  50.4 us
    all_gather x2, blocking collectives, per_device(): top_rows = lax.all_gather(adjoint[:, :, -1, :], 'lon', axis=2, tiled=True)  48.7 us
    ppermute x8, starting transfers between devices, padded(): lax.ppermute(head, axis, [((i + 1) % count, i) for i in range(ends)])  43.5 us
    dot_general x6, matrix products, closure(): jnp.dot(w_second.T, first, precision=HIGH) + b_second[:, None]  39.8 us
    dot_general x6, matrix products, closure(): jnp.dot(w_first.T, flat, precision=HIGH) + b_first[:, None]  30.9 us
    dot_general x4, matrix products, closure(): return jnp.dot(w_head, second, precision=HIGH) + b_head[0]  23.8 us
  transfers between devices with their start and end apart: 17, of which 3 were waited for; matrix products, arithmetic and copies ran while one was open for 14% of the time, Pallas kernels for 0%

commit v1 on v0

v1 whole, which is shorter than its diff:
```python
import math

import jax
import jax.numpy as jnp
from jax import lax
from jax.experimental import pallas as pl
from jax.experimental.pallas import tpu as pltpu
from jax.sharding import PartitionSpec as P

KMAX = 0.24
F32 = jnp.float32
BF16 = jnp.bfloat16
MESH = pl.DeviceIdType.MESH

NZ = 4
ROWS = 16
COLS = 128
HID = 128
FIELDS = 2 * NZ
CHUNKS = NZ * ROWS // 8
LANES = 8 * COLS
EAST, WEST, NORTH, SOUTH = 0, 1, 2, 3
OPPOSITE = (WEST, EAST, SOUTH, NORTH)


def halves(x):
    high = x.astype(BF16)
    return high, (x - high.astype(F32)).astype(BF16)


def dot(a, b):
    return jnp.dot(a, b, preferred_element_type=F32)


def dot_nt(a, b):
    return lax.dot_general(a, b, (((1,), (1,)), ((), ())), preferred_element_type=F32)


def lane_roll(x, by):
    flat = x.reshape(-1, COLS)
    return pltpu.roll(flat, by % COLS, 1).reshape(x.shape)


def column(row):
    return jnp.broadcast_to(row, (COLS, COLS)).T


def kernel(
    lat_count, lon_count, sub,
    tracers, land, levels, partner, cotangent, w_first, b_first, w_second, b_second, w_head, b_head,
    tracers_out, tracer_grad, gw_first, gw_second, gw_head,
    w1_rows, w1_fwd, w1_bwd, w2_fwd, w2_bwd, bias2, head,
    wet_ext, pair, state0, state1, adj0, adj1, kap0, kap1, contrast0, contrast1, coef0, coef1,
    slope0, slope1, direct, feats0, feats1, logits, h1_0, h1_1, h2_0, h2_1, dz2, dz1, dfeat,
    obar, acc2, acc1, acch,
    send0, send1, send2, recv0, recv1, recv2, fold0, fold1, fold2,
    parts, parts_lat, parts_lon, total, gathered,
    send_sem, recv_sem, fold_send, fold_recv, sum_send, sum_recv,
):
    lat = lax.axis_index("lat")
    lon = lax.axis_index("lon")
    at_top = lat == lat_count - 1
    at_bottom = lat == 0
    east = lax.rem(lon + 1, lon_count)
    west = lax.rem(lon + lon_count - 1, lon_count)

    barrier = pltpu.get_barrier_semaphore()
    for o in range(1, lat_count):
        pl.semaphore_signal(
            barrier, inc=1, device_id={"lat": lax.rem(lat + o, lat_count), "lon": lon},
            device_id_type=MESH,
        )
    for o in range(1, lon_count):
        pl.semaphore_signal(
            barrier, inc=1, device_id={"lat": lat, "lon": lax.rem(lon + o, lon_count)},
            device_id_type=MESH,
        )

    lane3 = lax.broadcasted_iota(jnp.int32, (FIELDS, ROWS, COLS), 2)
    lane8 = lax.broadcasted_iota(jnp.int32, (8, COLS), 1)
    sub8 = lax.broadcasted_iota(jnp.int32, (8, COLS), 0)

    def to_side(phase, side, sends, recvs):
        target = {
            EAST: {"lat": lat, "lon": east},
            WEST: {"lat": lat, "lon": west},
            NORTH: {"lat": jnp.minimum(lat + 1, lat_count - 1), "lon": lon},
            SOUTH: {"lat": jnp.maximum(lat - 1, 0), "lon": lon},
        }[side]
        back = OPPOSITE[side]
        return pltpu.make_async_remote_copy(
            src_ref=sends.at[side], dst_ref=recvs.at[back],
            send_sem=send_sem.at[phase, side], recv_sem=recv_sem.at[phase, back],
            device_id=target, device_id_type=MESH,
        )

    def start_phase(phase, sends, recvs, folds):
        to_side(phase, EAST, sends, recvs).start()
        to_side(phase, WEST, sends, recvs).start()

        @pl.when(jnp.logical_not(at_top))
        def _():
            to_side(phase, NORTH, sends, recvs).start()

        @pl.when(jnp.logical_not(at_bottom))
        def _():
            to_side(phase, SOUTH, sends, recvs).start()

        @pl.when(at_top)
        def _():
            for o in range(1, lon_count):
                pltpu.make_async_remote_copy(
                    src_ref=sends.at[NORTH], dst_ref=folds.at[lon],
                    send_sem=fold_send.at[phase], recv_sem=fold_recv.at[phase],
                    device_id={"lat": lat, "lon": lax.rem(lon + o, lon_count)},
                    device_id_type=MESH,
                ).start()
            folds[lon] = sends[NORTH]

    def wait_phase(phase, sends, recvs, folds):
        to_side(phase, WEST, sends, recvs).wait_recv()
        to_side(phase, EAST, sends, recvs).wait_recv()

        @pl.when(jnp.logical_not(at_top))
        def _():
            to_side(phase, SOUTH, sends, recvs).wait_recv()

        @pl.when(jnp.logical_not(at_bottom))
        def _():
            to_side(phase, NORTH, sends, recvs).wait_recv()

        @pl.when(at_top)
        def _():
            others = folds.at[pl.ds(0, lon_count - 1)]
            pltpu.make_async_copy(others, others, fold_recv.at[phase]).wait()
            block = jnp.broadcast_to(partner[...] >> 7, (8, COLS))
            lane = jnp.broadcast_to(partner[...] & (COLS - 1), (8, COLS))
            for g in range(sends.shape[1] // 8):
                rows = pl.ds(8 * g, 8)
                picked = jnp.zeros((8, COLS), F32)
                for j in range(lon_count):
                    taken = jnp.take_along_axis(folds[j, rows, :], lane, axis=1)
                    picked = jnp.where(block == j, taken, picked)
                recvs[NORTH, rows, :] = picked

    def finish_phase(phase, sends, recvs, folds):
        to_side(phase, EAST, sends, recvs).wait_send()
        to_side(phase, WEST, sends, recvs).wait_send()

        @pl.when(jnp.logical_not(at_top))
        def _():
            to_side(phase, NORTH, sends, recvs).wait_send()

        @pl.when(jnp.logical_not(at_bottom))
        def _():
            to_side(phase, SOUTH, sends, recvs).wait_send()

        @pl.when(at_top)
        def _():
            others = folds.at[pl.ds(0, lon_count - 1)]
            pltpu.make_async_copy(others, others, fold_send.at[phase]).wait()

    def pack(ext, sends, at):
        turned = ext[:, 8:24, :].reshape(COLS, COLS).T
        sends[EAST, at : at + 8, :] = turned[COLS - 8 :]
        sends[WEST, at : at + 8, :] = turned[:8]
        for i in range(FIELDS):
            sends[NORTH, at + i : at + i + 1, :] = ext[i, 23:24, :]
            sends[SOUTH, at + i : at + i + 1, :] = ext[i, 8:9, :]

    def unpack(ext, recvs, at):
        for i in range(FIELDS):
            ext[i, 24:25, :] = recvs[NORTH, at + i : at + i + 1, :]
            ext[i, 7:8, :] = recvs[SOUTH, at + i : at + i + 1, :]

    def edge_columns(recvs, at):
        from_east = column(recvs[EAST, at : at + 1, :]).reshape(FIELDS, ROWS, COLS)
        from_west = column(recvs[WEST, at + 7 : at + 8, :]).reshape(FIELDS, ROWS, COLS)
        return from_east, from_west

    def sides(ext, from_east, from_west):
        core = ext[:, 8:24, :]
        lane = lane3[: core.shape[0]]
        return [
            jnp.where(lane == COLS - 1, from_east, lane_roll(core, -1)),
            jnp.where(lane == 0, from_west, lane_roll(core, 1)),
            ext[:, 9:25, :],
            ext[:, 7:23, :],
        ]

    def store_feature(feats, chunk, f, value):
        feats[chunk, pl.ds(f, 8, stride=8), :] = value

    def own_features(ext, feats):
        for half in range(2):
            rows = pl.ds(8 + 8 * half, 8)
            wets = [wet_ext[k, rows, :] for k in range(NZ)]
            for t in range(2):
                cells = [ext[NZ * t + k, rows, :] for k in range(NZ)]
                vertical = [
                    (cells[k + 1] - cells[k]) * (wets[k + 1] * wets[k]) for k in range(NZ - 1)
                ]
                zero = jnp.zeros((8, COLS), F32)
                for k in range(NZ):
                    chunk = 2 * k + half
                    store_feature(feats, chunk, t, cells[k])
                    store_feature(feats, chunk, 2 + t, -vertical[k - 1] if k > 0 else zero)
                    store_feature(feats, chunk, 4 + t, vertical[k] if k < NZ - 1 else zero)

    def halo_features(recvs, feats):
        north, south = recvs[NORTH, 0:8, :], recvs[SOUTH, 0:8, :]
        first = sub8 < NZ
        wet = jnp.where(first, recv0[NORTH, 16:24, :], pltpu.roll(recv0[SOUTH, 16:24, :], 4, 0))
        joint = jnp.where(
            lax.rem(sub8, NZ) == NZ - 1, 0.0, wet * pltpu.roll(wet, 7, 0)
        )
        fields = (
            jnp.where(first, north, pltpu.roll(south, 4, 0)),
            jnp.where(first, pltpu.roll(north, 4, 0), south),
        )
        for t, cells in enumerate(fields):
            vertical = (pltpu.roll(cells, 7, 0) - cells) * joint
            store_feature(feats, CHUNKS, t, cells)
            store_feature(feats, CHUNKS, 2 + t, -pltpu.roll(vertical, 1, 0))
            store_feature(feats, CHUNKS, 4 + t, vertical)
        east_row = jnp.broadcast_to(recvs[EAST, 0:1, :], (8, COLS))
        west_row = jnp.broadcast_to(recvs[WEST, 7:8, :], (8, COLS))
        first = lane8 < NZ * ROWS
        wet_col = edge_wet()
        joint = jnp.where(
            lax.rem(lane8, NZ * ROWS) >= (NZ - 1) * ROWS, 0.0,
            wet_col * pltpu.roll(wet_col, COLS - ROWS, 1),
        )
        fields = (
            jnp.where(first, east_row, pltpu.roll(west_row, NZ * ROWS, 1)),
            jnp.where(first, pltpu.roll(east_row, NZ * ROWS, 1), west_row),
        )
        for t, cells in enumerate(fields):
            vertical = (pltpu.roll(cells, COLS - ROWS, 1) - cells) * joint
            feats[CHUNKS + 1, t : t + 1, :] = cells[0:1]
            feats[CHUNKS + 1, 2 + t : 3 + t, :] = -pltpu.roll(vertical, ROWS, 1)[0:1]
            feats[CHUNKS + 1, 4 + t : 5 + t, :] = vertical[0:1]
        return wet

    def edge_wet():
        wet_east = jnp.broadcast_to(recv0[EAST, 16:17, :], (8, COLS))
        wet_west = jnp.broadcast_to(recv0[WEST, 23:24, :], (8, COLS))
        return jnp.where(lane8 < NZ * ROWS, wet_east, wet_west)

    def wide(x, n):
        return jnp.concatenate([x] * n, axis=1) if n > 1 else x

    def closure_chunk(feats, chunk, rows, h1_ref, h2_ref):
        for s in range(0, rows, sub):
            n = min(sub, rows - s)
            f = [feats[chunk, 8 * (s + q) : 8 * (s + q) + 8, :] for q in range(n)]
            f = jnp.concatenate(f, axis=1) if n > 1 else f[0]
            high = f.astype(BF16).astype(F32)
            low = f - high
            stacked = jnp.concatenate([high, low, high, low], axis=0).astype(BF16)
            h1 = jnp.tanh(dot(w1_fwd[...], stacked))
            h1_high, h1_low = halves(h1)
            pre2 = dot(w2_fwd[...], jnp.concatenate([h1_high, h1_low, h1_high], axis=0))
            h2 = jnp.tanh(pre2 + wide(bias2[...], n))
            o = jnp.sum(h2 * wide(head[...], n), axis=0, keepdims=True)
            for q in range(n):
                logits[chunk, s + q : s + q + 1, :] = o[:, COLS * q : COLS * (q + 1)]
            if h1_ref is not None:
                lanes = slice(COLS * s, COLS * (s + n))
                h1_ref[chunk, :HID, lanes] = h1_high
                h1_ref[chunk, HID:, lanes] = h1_low
                h2_ref[chunk, :, lanes] = h2

    def closure_own(feats, h1_ref, h2_ref):
        @pl.loop(0, CHUNKS)
        def _(chunk):
            closure_chunk(feats, chunk, 8, h1_ref, h2_ref)

    def kappa_from(o, wet):
        gate = jax.nn.sigmoid(o + b_head[0])
        return KMAX * gate * wet, KMAX * gate * (1.0 - gate) * wet

    def advance(phase, state, feats, sends, recvs, folds, h1_ref, h2_ref, kap, slope, contrast, coef):
        own_features(state, feats)
        closure_own(feats, h1_ref, h2_ref)
        wait_phase(phase, sends, recvs, folds)
        unpack(state, recvs, 0)
        if phase == 0:
            unpack(adj0, recvs, 8)
            unpack(wet_ext, recvs, 16)
            wet_east, wet_west = edge_columns(recvs, 16)
            wet = wet_ext[:NZ, 8:24, :]
            around = sides(wet_ext, wet_east, wet_west)
            for n in range(4):
                pair[n] = 0.5 * wet * around[n][:NZ]
        wet_halo = halo_features(recvs, feats)
        closure_chunk(feats, CHUNKS, 8, None, None)
        closure_chunk(feats, CHUNKS + 1, 1, None, None)
        for k in range(NZ):
            for half in range(2):
                rows = pl.ds(8 + 8 * half, 8)
                value, rise = kappa_from(logits[2 * k + half], wet_ext[k, rows, :])
                kap[k, rows, :] = value
                slope[2 * k + half] = rise
        value, _ = kappa_from(logits[CHUNKS], wet_halo)
        for k in range(NZ):
            kap[k, 24:25, :] = value[k : k + 1]
            kap[k, 7:8, :] = value[NZ + k : NZ + k + 1]
        value, _ = kappa_from(logits[CHUNKS + 1], edge_wet())
        kap_edges = column(value[0:1]).reshape(2, NZ, ROWS, COLS)
        kap_sides = sides(kap, kap_edges[0], kap_edges[1])
        tracer_sides = sides(state, *edge_columns(recvs, 0))
        core = state[:, 8:24, :]
        own_kap = kap[:, 8:24, :]
        change = jnp.zeros_like(core)
        for n in range(4):
            difference = tracer_sides[n] - core
            weight = (own_kap + kap_sides[n]) * pair[n]
            contrast[n] = difference
            coef[n] = weight
            change = change + jnp.concatenate([weight, weight], 0) * difference
        return core + change

    def pull_flux(adjoint, recvs, at, contrast, coef, slope):
        core = adjoint[:, 8:24, :]
        around = sides(adjoint, *edge_columns(recvs, at))
        total_direct = core
        kappa_bar = jnp.zeros((NZ, ROWS, COLS), F32)
        for n in range(4):
            difference = around[n] - core
            weight = coef[n]
            total_direct = total_direct + jnp.concatenate([weight, weight], 0) * difference
            product = contrast[n] * difference
            kappa_bar = kappa_bar - pair[n] * (product[:NZ] + product[NZ:])
        direct[...] = total_direct
        obar[...] = kappa_bar.reshape(CHUNKS, 8, COLS) * slope[...]

    def pull_closure(h1_ref, h2_ref):
        @pl.loop(0, CHUNKS)
        def _(chunk):
            heads = jnp.zeros((HID, COLS), F32)
            for s in range(0, 8, sub):
                n = min(sub, 8 - s)
                lanes = slice(COLS * s, COLS * (s + n))
                bar = [obar[chunk, s + q : s + q + 1, :] for q in range(n)]
                bar = jnp.concatenate(bar, axis=1) if n > 1 else bar[0]
                h2 = h2_ref[chunk, :, lanes]
                weighted = h2 * bar
                for q in range(n):
                    heads = heads + weighted[:, COLS * q : COLS * (q + 1)]
                d2_high, d2_low = halves(wide(head[...], n) * (bar - weighted * h2))
                dh1 = dot(w2_bwd[...], jnp.concatenate([d2_high, d2_low, d2_high], axis=0))
                h1 = h1_ref[chunk, :HID, lanes].astype(F32) + h1_ref[chunk, HID:, lanes].astype(F32)
                d1_high, d1_low = halves(dh1 * (1.0 - h1 * h1))
                dz2[chunk, :HID, lanes] = d2_high
                dz2[chunk, HID:, lanes] = d2_low
                dz1[chunk, :HID, lanes] = d1_high
                dz1[chunk, HID:, lanes] = d1_low
            acch[...] += heads

    def pull_features():
        @pl.loop(0, CHUNKS)
        def _(chunk):
            d1 = dz1[chunk]
            d = dot(w1_bwd[...], jnp.concatenate([d1, d1[:HID]], axis=0))
            for q in range(8):
                dfeat[chunk, 8 * q : 8 * q + 8, :] = d[:8, COLS * q : COLS * (q + 1)]

    def add_weights(feats, h1_ref):
        @pl.loop(0, CHUNKS)
        def _(chunk):
            acc2[...] += dot_nt(h1_ref[chunk], dz2[chunk])
            f = jnp.concatenate([feats[chunk, 8 * q : 8 * q + 8, :] for q in range(8)], axis=1)
            high = f.astype(BF16).astype(F32)
            stacked = jnp.concatenate([high, f - high], axis=0).astype(BF16)
            acc1[...] += dot_nt(stacked, dz1[chunk])

    def pull_state(store):
        for half in range(2):
            rows = pl.ds(8 * half, 8)
            wets = [wet_ext[k, pl.ds(8 + 8 * half, 8), :] for k in range(NZ)]
            for t in range(2):
                bar = [
                    [dfeat[2 * k + half, pl.ds(f, 8, stride=8), :] for k in range(NZ)]
                    for f in (t, 2 + t, 4 + t)
                ]
                vertical = [
                    (bar[2][k] - bar[1][k + 1]) * (wets[k + 1] * wets[k]) for k in range(NZ - 1)
                ]
                for k in range(NZ):
                    value = direct[NZ * t + k, rows, :] + bar[0][k]
                    if k < NZ - 1:
                        value = value - vertical[k]
                    if k > 0:
                        value = value + vertical[k - 1]
                    store(NZ * t + k, half, value)

    depth_here = land[...] * levels[...]
    for k in range(NZ):
        wet = (k < depth_here).astype(F32)
        wet_ext[k, 8:24, :] = wet
        wet_ext[NZ + k, 8:24, :] = wet
    state0[:, 8:24, :] = tracers[...]
    adj0[:, 8:24, :] = cotangent[...]
    pack(state0, send0, 0)
    pack(adj0, send0, 8)
    pack(wet_ext, send0, 16)

    @pl.when(at_bottom)
    def _():
        for recvs in (recv0, recv1, recv2):
            recvs[SOUTH] = jnp.zeros(recvs.shape[1:], F32)

    pl.semaphore_wait(barrier, lat_count + lon_count - 2)
    start_phase(0, send0, recv0, fold0)

    w1_rows[0:6, :] = w_first[...]
    w1_rows[6:7, :] = b_first[...]
    w1_rows[7:8, :] = jnp.zeros((1, HID), F32)
    w1 = w1_rows[...]
    w1_high = w1.astype(BF16).astype(F32)
    w1_low = w1 - w1_high
    tall = jnp.concatenate(
        [w1_high, w1_high, w1_low, w1_low, jnp.zeros((HID - 32, HID), F32)], axis=0
    )
    w1_fwd[...] = tall.T[:, :32].astype(BF16)
    blank = jnp.zeros((8, HID), F32)
    w1_high = jnp.concatenate([w1_high, blank], axis=0).astype(BF16)
    w1_low = jnp.concatenate([w1_low, blank], axis=0).astype(BF16)
    w1_bwd[...] = jnp.concatenate([w1_high, w1_high, w1_low], axis=1)
    w2 = w_second[...]
    high, low = halves(w2)
    w2_bwd[...] = jnp.concatenate([high, high, low], axis=1)
    high, low = halves(w2.T)
    w2_fwd[...] = jnp.concatenate([high, high, low], axis=1)
    bias2[...] = column(b_second[...])
    head[...] = column(w_head[...])
    ones_row = jnp.where(sub8 == 6, 1.0, 0.0)
    for feats in (feats0, feats1):
        for chunk in range(CHUNKS + 1):
            feats[chunk, pl.ds(6, 8, stride=8), :] = jnp.ones((8, COLS), F32)
            feats[chunk, pl.ds(7, 8, stride=8), :] = jnp.zeros((8, COLS), F32)
        feats[CHUNKS + 1, 0:8, :] = ones_row
    logits[CHUNKS + 1] = jnp.zeros((8, COLS), F32)
    acc2[...] = jnp.zeros_like(acc2)
    acc1[...] = jnp.zeros_like(acc1)
    acch[...] = jnp.zeros_like(acch)

    state1[:, 8:24, :] = advance(
        0, state0, feats0, send0, recv0, fold0, h1_0, h2_0, kap0, slope0, contrast0, coef0
    )
    pack(state1, send1, 0)
    start_phase(1, send1, recv1, fold1)
    tracers_out[...] = advance(
        1, state1, feats1, send1, recv1, fold1, h1_1, h2_1, kap1, slope1, contrast1, coef1
    )

    pull_flux(adj0, recv0, 8, contrast1, coef1, slope1)
    pull_closure(h1_1, h2_1)
    pull_features()

    def keep(i, half, value):
        adj1[i, 8 + 8 * half : 16 + 8 * half, :] = value

    pull_state(keep)
    pack(adj1, send2, 0)
    start_phase(2, send2, recv2, fold2)
    add_weights(feats1, h1_1)
    wait_phase(2, send2, recv2, fold2)
    unpack(adj1, recv2, 0)
    pull_flux(adj1, recv2, 0, contrast0, coef0, slope0)
    pull_closure(h1_0, h2_0)
    add_weights(feats0, h1_0)

    piece = HID // lat_count
    both = piece + 8
    second = (
        (acc2[HID:, HID:] + acc2[HID:, :HID]) + acc2[:HID, HID:]
    ) + acc2[:HID, :HID]
    first = (acc1[8:, :HID] + acc1[:8, HID:]) + acc1[:8, :HID]
    head_row = jnp.sum(acch[...].T, axis=0, keepdims=True)
    extra = jnp.where(sub8 == 6, jnp.broadcast_to(head_row, (8, COLS)), first)
    for p in range(lat_count):
        parts[p, :piece, :] = second[piece * p : piece * (p + 1)]
        parts[p, piece:, :] = extra

    def lat_copy(o, src, dst, step):
        return pltpu.make_async_remote_copy(
            src_ref=src, dst_ref=dst, send_sem=sum_send.at[step], recv_sem=sum_recv.at[step],
            device_id={"lat": lax.rem(lat + o, lat_count), "lon": lon}, device_id_type=MESH,
        )

    def lon_copy(o, src, dst, step):
        return pltpu.make_async_remote_copy(
            src_ref=src, dst_ref=dst, send_sem=sum_send.at[step], recv_sem=sum_recv.at[step],
            device_id={"lat": lat, "lon": lax.rem(lon + o, lon_count)}, device_id_type=MESH,
        )

    def wait_all(ref, count, sem):
        some = ref.at[pl.ds(0, count)]
        pltpu.make_async_copy(some, some, sem).wait()

    for o in range(1, lat_count):
        lat_copy(o, parts.at[lax.rem(lat + o, lat_count)], parts_lat.at[lat], 0).start()
    parts_lat[lat] = parts[lat]

    pull_features()

    def finish(i, half, value):
        tracer_grad[i, 8 * half : 8 * half + 8, :] = value

    pull_state(finish)

    wait_all(parts_lat, lat_count - 1, sum_recv.at[0])
    summed = parts_lat[0]
    for p in range(1, lat_count):
        summed = summed + parts_lat[p]
    parts_lon[lon] = summed
    for o in range(1, lon_count):
        lon_copy(o, parts_lon.at[lon], parts_lon.at[lon], 1).start()
    wait_all(parts_lon, lon_count - 1, sum_recv.at[1])
    summed = parts_lon[0]
    for p in range(1, lon_count):
        summed = summed + parts_lon[p]
    cells_all = lat_count * ROWS * lon_count * COLS * NZ
    summed = summed * (1.0 / math.sqrt(cells_all))
    gathered[lat] = summed[:piece]
    for o in range(1, lat_count):
        lat_copy(o, gathered.at[lat], gathered.at[lat], 2).start()
    gw_first[...] = summed[piece : piece + 6]
    gw_head[...] = summed[piece + 6 : piece + 7]
    wait_all(gathered, lat_count - 1, sum_recv.at[2])
    for p in range(lat_count):
        gw_second[piece * p : piece * (p + 1), :] = gathered[p]

    finish_phase(0, send0, recv0, fold0)
    finish_phase(1, send1, recv1, fold1)
    finish_phase(2, send2, recv2, fold2)
    wait_all(parts_lat, lat_count - 1, sum_send.at[0])
    wait_all(parts_lon, lon_count - 1, sum_send.at[1])
    wait_all(gathered, lat_count - 1, sum_send.at[2])


def per_device(lat_count, lon_count, sub, tracers, land_mask, level_counts, fold_partner, cotangent,
               w_first, b_first, w_second, b_second, w_head, b_head):
    field = (FIELDS, ROWS, COLS)
    ext = pltpu.VMEM((FIELDS, 32, COLS), F32)
    kap = pltpu.VMEM((NZ, 32, COLS), F32)
    feats = pltpu.VMEM((CHUNKS + 2, 64, COLS), F32)
    stack = pltpu.VMEM((CHUNKS, 2 * HID, LANES), BF16)
    dense = pltpu.VMEM((CHUNKS, HID, LANES), F32)
    tile = pltpu.VMEM((CHUNKS, 8, COLS), F32)
    piece = HID // lat_count
    both = piece + 8
    scratch = [
        pltpu.VMEM((8, HID), F32),
        pltpu.VMEM((HID, 32), BF16),
        pltpu.VMEM((16, 3 * HID), BF16),
        pltpu.VMEM((HID, 3 * HID), BF16),
        pltpu.VMEM((HID, 3 * HID), BF16),
        pltpu.VMEM((HID, COLS), F32),
        pltpu.VMEM((HID, COLS), F32),
        ext,
        pltpu.VMEM((4, NZ, ROWS, COLS), F32),
        ext, ext, ext, ext, kap, kap,
        pltpu.VMEM((4,) + field, F32),
        pltpu.VMEM((4,) + field, F32),
        pltpu.VMEM((4, NZ, ROWS, COLS), F32),
        pltpu.VMEM((4, NZ, ROWS, COLS), F32),
        tile, tile,
        pltpu.VMEM(field, F32),
        feats, feats,
        pltpu.VMEM((CHUNKS + 2, 8, COLS), F32),
        stack, stack, dense, dense, stack, stack,
        pltpu.VMEM((CHUNKS, 64, COLS), F32),
        tile,
        pltpu.VMEM((2 * HID, 2 * HID), F32),
        pltpu.VMEM((16, 2 * HID), F32),
        pltpu.VMEM((HID, COLS), F32),
    ]
    scratch += [pltpu.VMEM((4, n, COLS), F32) for n in (24, 8, 8)] * 2
    scratch += [pltpu.VMEM((lon_count, n, COLS), F32) for n in (24, 8, 8)]
    scratch += [
        pltpu.VMEM((lat_count, both, COLS), F32),
        pltpu.VMEM((lat_count, both, COLS), F32),
        pltpu.VMEM((lon_count, both, COLS), F32),
        pltpu.VMEM((8, COLS), F32),
        pltpu.VMEM((lat_count, piece, COLS), F32),
        pltpu.SemaphoreType.DMA((3, 4)),
        pltpu.SemaphoreType.DMA((3, 4)),
        pltpu.SemaphoreType.DMA((3,)),
        pltpu.SemaphoreType.DMA((3,)),
        pltpu.SemaphoreType.DMA((3,)),
        pltpu.SemaphoreType.DMA((3,)),
    ]
    vmem = pl.BlockSpec(memory_space=pltpu.VMEM)
    run = pl.pallas_call(
        lambda *refs: kernel(lat_count, lon_count, sub, *refs),
        out_shape=[
            jax.ShapeDtypeStruct(field, F32),
            jax.ShapeDtypeStruct(field, F32),
            jax.ShapeDtypeStruct((6, HID), F32),
            jax.ShapeDtypeStruct((HID, HID), F32),
            jax.ShapeDtypeStruct((1, HID), F32),
        ],
        in_specs=[vmem] * 10 + [pl.BlockSpec(memory_space=pltpu.SMEM)],
        out_specs=[vmem] * 5,
        scratch_shapes=scratch,
        compiler_params=pltpu.CompilerParams(
            collective_id=0, has_side_effects=True, vmem_limit_bytes=56 * 2**20
        ),
        name="adjoint_steps",
    )
    out, grad, first, second, head = run(
        tracers.reshape(field), land_mask, level_counts, fold_partner.reshape(1, COLS),
        cotangent.reshape(field), w_first, b_first.reshape(1, HID), w_second,
        b_second.reshape(1, HID), w_head.reshape(1, HID), b_head,
    )
    return (
        out.reshape(tracers.shape), grad.reshape(tracers.shape), first, second, head.reshape(HID)
    )


def solution(mesh):
    lat_count, lon_count = mesh.shape["lat"], mesh.shape["lon"]
    grid = P(None, None, "lat", "lon")
    return jax.shard_map(
        lambda *args: per_device(lat_count, lon_count, 2, *args),
        mesh=mesh,
        in_specs=(
            grid, P("lat", "lon"), P("lat", "lon"), P("lon"), grid,
            P(), P(), P(), P(), P(), P(),
        ),
        out_specs=(grid, grid, P(), P(), P()),
        check_vma=False,
    )
```

time: 570 us -> 64.1 us (0.11); the launches traced: 559 us -> 63.9 us
  blocking collectives: 182 us -> 0 us
  waiting for transfers between devices: 152 us -> 0 us
  matrix products: 94.5 us -> 0 us
  starting transfers between devices: 59.4 us -> 0 us
  Pallas kernels: 0 us -> 58.7 us
  local copies, waits for them, and re-layouts: 35.4 us -> 3.93 us
  other arithmetic: 20.5 us -> 0 us
  between operations: 15.9 us -> 1.3 us
    psum x1 -> x0, waiting for transfers between devices: 145 us -> none  [per_device(): totals = lax.psum(totals, ('lon', 'lat'))]
    all_gather x4 -> x0, blocking collectives: 99.1 us -> none  [the longest x2 50.4 us: per_device(): top_rows = lax.all_gather(payload[:, :, -1, :], 'lon', axis=2, tiled=True)]
    dot_general x16 -> x0, matrix products: 94.5 us -> none  [the longest x6 39.8 us: closure(): jnp.dot(w_second.T, first, precision=HIGH) + b_second[:, None]]
    psum x1 -> x0, blocking collectives: 83 us -> none  [per_device(): totals = lax.psum(totals, ('lon', 'lat'))]
    ppermute x16 -> x0, starting transfers between devices: 59.4 us -> none  [the longest x8 43.5 us: padded(): lax.ppermute(head, axis, [((i + 1) % count, i) for i in range(ends)])]
    pallas_call x0 -> x1, Pallas kernels: none -> 58.7 us  [per_device(): run(tracers.reshape(field), land_mask, level_counts, fold_partner.reshape...]
    gather x8 -> x0, local copies, waits for them, and re-layouts: 11.7 us -> none  [per_device(): fold_row = jnp.take(top_rows, fold_partner, axis=2)]
    all_gather x4 -> x0, local copies, waits for them, and re-layouts: 8.43 us -> none  [the longest x2 6.27 us: per_device(): top_rows = lax.all_gather(payload[:, :, -1, :], 'lon', axis=2, tiled=True)]
  transfers between devices with their start and end apart: 17 -> 0, of which waited for: 3 -> 0; matrix products, arithmetic and copies ran while one was open for 14% -> 0% of each run, Pallas kernels for 0% -> 0%
where the time goes in v1:
time: 64.1 us; the launch traced here: 63.9 us
  Pallas kernels  58.7 us (92%)
  local copies, waits for them, and re-layouts  3.93 us (6%)
  between operations  1.3 us (2%)
    pallas_call x1, Pallas kernels, per_device(): run(tracers.reshape(field), land_mask, level_counts, fold_partner.reshape...  58.7 us
    unnamed x13, local copies, waits for them, and re-layouts  3.93 us

profile of v1, /device:TPU:1, one launch (start us, length us, event | category | flops | bytes accessed | tf_op | source)
XLA Modules:
  0.0 63.9 jit_solution(15306031360973727219)
XLA Ops:
  1.3 58.7 %adjoint_steps.1 = (f32[8,16,128]{2,1,0:T(8,128)}, f32[8,16,128]{2,1,0:T(8,128)}, f32[6,128]{1,0:T(8,128)}, f32[128,128]{1,0:T(8,128)}, f32[1,128]{1,0:T(1,128)}) custom-call(f32[8,16,128]{2,1,0:T(8,128)} %bitcast.9, s32[16,128]{1,0:T(8,128)} %refs_1_.1, s32[16,128]{1,0:T(8,128)} %refs_2_.1, s32[1,128]{1,0:T(1,128)} %bitcast.13, f32[8,16,128]{2,1,0:T(8,128)} %bitcast.10, ...), custom_call_target="tpu_custom_call" | custom-call | tf_op jit(solution)/shard_map/adjoint_steps/pallas_call | solution.py:614
  59.9 0.0 copy-start.1
  60.0 1.5 %copy.22 = f32[2,4,16,128]{3,2,1,0:T(8,128)} copy(f32[2,4,16,128]{3,2,1,0:T(8,128)} %bitcast.12) | data formatting | bytes 131072
  61.5 0.0 copy-done.1
  61.5 0.0 copy-start.2
  61.5 0.0 copy-start
  61.5 0.6 copy.23
  62.1 0.1 copy-done.2
  62.1 0.6 copy.24
  62.7 0.0 copy-done
  62.7 0.0 copy-start.3
  62.7 0.6 copy.25
  63.4 0.0 copy-done.3
  63.4 0.5 copy.26
Async XLA Ops:
  59.9 1.5 %copy-start.1 = (f32[8,16,128]{2,1,0:T(8,128)S(1)}, f32[8,16,128]{2,1,0:T(8,128)}, u32[]{:S(2)}) copy-start(f32[8,16,128]{2,1,0:T(8,128)} %get-tuple-element.11) | copy-start | bytes 196612
  61.5 0.7 %copy-start.2 = (f32[6,128]{1,0:T(8,128)S(1)}, f32[6,128]{1,0:T(8,128)}, u32[]{:S(2)}) copy-start(f32[6,128]{1,0:T(8,128)} %get-tuple-element.22) | copy-start | bytes 9220
  61.5 1.3 %copy-start = (f32[128,128]{1,0:T(8,128)S(1)}, f32[128,128]{1,0:T(8,128)}, u32[]{:S(2)}) copy-start(f32[128,128]{1,0:T(8,128)} %get-tuple-element.23) | copy-start | bytes 196612
  62.7 0.6 copy-start.3

commit v2 on v1

--- a/solution.py
+++ b/solution.py
@@ -23,6 +23,33 @@
 OPPOSITE = (WEST, EAST, SOUTH, NORTH)
 
 
+PLANE = ("x", "y_high", "y_low")
+PILLAR = ("core", "z")
+
+
+def place_sizes(lat_count, lon_count):
+    if lat_count == 16 and lon_count == 16:
+        return {"core": 2, "x": 4, "y_high": 2, "y_low": 2, "z": 8}
+    return {"core": 1, "x": lat_count, "y_high": 1, "y_low": 1, "z": lon_count}
+
+
+def offsets(dims, sizes):
+    steps = [{}]
+    for d in dims:
+        steps = [{**s, d: o} for s in steps for o in range(sizes[d])]
+
+    def hops(s):
+        y = {(0, 0): 0, (1, 0): 2, (0, 1): 1, (1, 1): 1}[s.get("y_high", 0), s.get("y_low", 0)]
+        x, z = s.get("x", 0), s.get("z", 0)
+        return y + min(x, sizes["x"] - x) + min(z, sizes["z"] - z)
+
+    return sorted([s for s in steps if any(s.values())], key=hops, reverse=True)
+
+
+def piece_rows(parts):
+    return HID // parts, -(-8 // parts)
+
+
 def halves(x):
     high = x.astype(BF16)
     return high, (x - high.astype(F32)).astype(BF16)
@@ -54,8 +81,8 @@
     slope0, slope1, direct, feats0, feats1, logits, h1_0, h1_1, h2_0, h2_1, dz2, dz1, dfeat,
     obar, acc2, acc1, acch,
     send0, send1, send2, recv0, recv1, recv2, fold0, fold1, fold2,
-    parts, parts_lat, parts_lon, total, gathered,
-    send_sem, recv_sem, fold_send, fold_recv, sum_send, sum_recv,
+    parts, parts_plane, parts_pillar, gathered, extras,
+    send_sem, recv_sem, fold_send, fold_recv, sum_send, sum_recv, in_sem,
 ):
     lat = lax.axis_index("lat")
     lon = lax.axis_index("lon")
@@ -64,17 +91,57 @@
     east = lax.rem(lon + 1, lon_count)
     west = lax.rem(lon + lon_count - 1, lon_count)
 
+    sizes = place_sizes(lat_count, lon_count)
+    core_count, x_count, y_low_count = sizes["core"], sizes["x"], sizes["y_low"]
+    here = {
+        "core": lax.rem(lat, core_count),
+        "x": lax.rem(lax.div(lat, core_count), x_count),
+        "y_high": lax.div(lat, core_count * x_count),
+        "y_low": lax.rem(lon, y_low_count),
+        "z": lax.div(lon, y_low_count),
+    }
+
+    def device_at(at):
+        return {
+            "lat": (at["y_high"] * x_count + at["x"]) * core_count + at["core"],
+            "lon": at["z"] * y_low_count + at["y_low"],
+        }
+
+    def moved(offset):
+        return {d: lax.rem(here[d] + offset.get(d, 0), sizes[d]) for d in here}
+
+    def slot(dims, at):
+        index = 0
+        for d in dims:
+            index = index * sizes[d] + at[d]
+        return index
+
     barrier = pltpu.get_barrier_semaphore()
-    for o in range(1, lat_count):
-        pl.semaphore_signal(
-            barrier, inc=1, device_id={"lat": lax.rem(lat + o, lat_count), "lon": lon},
-            device_id_type=MESH,
-        )
-    for o in range(1, lon_count):
-        pl.semaphore_signal(
-            barrier, inc=1, device_id={"lat": lat, "lon": lax.rem(lon + o, lon_count)},
-            device_id_type=MESH,
-        )
+
+    def greet(device):
+        pl.semaphore_signal(barrier, inc=1, device_id=device, device_id_type=MESH)
+
+    greeted = 4
+    greet({"lat": lat, "lon": east})
+    greet({"lat": lat, "lon": west})
+    greet({"lat": lax.rem(lat + 1, lat_count), "lon": lon})
+    greet({"lat": lax.rem(lat + lat_count - 1, lat_count), "lon": lon})
+    for dims in (PLANE, PILLAR):
+        for offset in offsets(dims, sizes):
+            greet(device_at(moved(offset)))
+            greeted += 1
+
+    @pl.when(at_top)
+    def _():
+        for o in range(1, lon_count):
+            greet({"lat": lat, "lon": lax.rem(lon + o, lon_count)})
+
+    loads = [
+        pltpu.make_async_copy(tracers, state0.at[:, pl.ds(8, ROWS), :], in_sem.at[0]),
+        pltpu.make_async_copy(cotangent, adj0.at[:, pl.ds(8, ROWS), :], in_sem.at[1]),
+    ]
+    for load in loads:
+        load.start()
 
     lane3 = lax.broadcasted_iota(jnp.int32, (FIELDS, ROWS, COLS), 2)
     lane8 = lax.broadcasted_iota(jnp.int32, (8, COLS), 1)
@@ -164,26 +231,25 @@
         turned = ext[:, 8:24, :].reshape(COLS, COLS).T
         sends[EAST, at : at + 8, :] = turned[COLS - 8 :]
         sends[WEST, at : at + 8, :] = turned[:8]
-        for i in range(FIELDS):
-            sends[NORTH, at + i : at + i + 1, :] = ext[i, 23:24, :]
-            sends[SOUTH, at + i : at + i + 1, :] = ext[i, 8:9, :]
+        sends[NORTH, at : at + 8, :] = ext[:, 23, :]
+        sends[SOUTH, at : at + 8, :] = ext[:, 8, :]
 
     def unpack(ext, recvs, at):
-        for i in range(FIELDS):
-            ext[i, 24:25, :] = recvs[NORTH, at + i : at + i + 1, :]
-            ext[i, 7:8, :] = recvs[SOUTH, at + i : at + i + 1, :]
+        ext[:, 24, :] = recvs[NORTH, at : at + 8, :]
+        ext[:, 7, :] = recvs[SOUTH, at : at + 8, :]
 
     def edge_columns(recvs, at):
-        from_east = column(recvs[EAST, at : at + 1, :]).reshape(FIELDS, ROWS, COLS)
-        from_west = column(recvs[WEST, at + 7 : at + 8, :]).reshape(FIELDS, ROWS, COLS)
-        return from_east, from_west
-
-    def sides(ext, from_east, from_west):
+        first = pltpu.roll(recvs[WEST, at : at + 8, :], 1, 0)
+        last = pltpu.roll(recvs[EAST, at : at + 8, :], 7, 0)
+        middle = jnp.zeros((COLS - 16, COLS), F32)
+        return jnp.concatenate([first, middle, last], axis=0).T.reshape(FIELDS, ROWS, COLS)
+
+    def sides(ext, edges):
         core = ext[:, 8:24, :]
         lane = lane3[: core.shape[0]]
         return [
-            jnp.where(lane == COLS - 1, from_east, lane_roll(core, -1)),
-            jnp.where(lane == 0, from_west, lane_roll(core, 1)),
+            jnp.where(lane == COLS - 1, edges, lane_roll(core, -1)),
+            jnp.where(lane == 0, edges, lane_roll(core, 1)),
             ext[:, 9:25, :],
             ext[:, 7:23, :],
         ]
@@ -272,7 +338,7 @@
                 h2_ref[chunk, :, lanes] = h2
 
     def closure_own(feats, h1_ref, h2_ref):
-        @pl.loop(0, CHUNKS)
+        @pl.loop(0, CHUNKS, unroll=CHUNKS)
         def _(chunk):
             closure_chunk(feats, chunk, 8, h1_ref, h2_ref)
 
@@ -288,9 +354,8 @@
         if phase == 0:
             unpack(adj0, recvs, 8)
             unpack(wet_ext, recvs, 16)
-            wet_east, wet_west = edge_columns(recvs, 16)
             wet = wet_ext[:NZ, 8:24, :]
-            around = sides(wet_ext, wet_east, wet_west)
+            around = sides(wet_ext, edge_columns(recvs, 16))
             for n in range(4):
                 pair[n] = 0.5 * wet * around[n][:NZ]
         wet_halo = halo_features(recvs, feats)
@@ -307,9 +372,11 @@
             kap[k, 24:25, :] = value[k : k + 1]
             kap[k, 7:8, :] = value[NZ + k : NZ + k + 1]
         value, _ = kappa_from(logits[CHUNKS + 1], edge_wet())
-        kap_edges = column(value[0:1]).reshape(2, NZ, ROWS, COLS)
-        kap_sides = sides(kap, kap_edges[0], kap_edges[1])
-        tracer_sides = sides(state, *edge_columns(recvs, 0))
+        same = jnp.broadcast_to(value[0:1], (8, COLS))
+        middle = jnp.zeros((COLS - 16, COLS), F32)
+        kap_edges = jnp.concatenate([pltpu.roll(same, NZ * ROWS, 1), middle, same], axis=0).T
+        kap_sides = sides(kap, kap_edges[: NZ * ROWS].reshape(NZ, ROWS, COLS))
+        tracer_sides = sides(state, edge_columns(recvs, 0))
         core = state[:, 8:24, :]
         own_kap = kap[:, 8:24, :]
         change = jnp.zeros_like(core)
@@ -323,7 +390,7 @@
 
     def pull_flux(adjoint, recvs, at, contrast, coef, slope):
         core = adjoint[:, 8:24, :]
-        around = sides(adjoint, *edge_columns(recvs, at))
+        around = sides(adjoint, edge_columns(recvs, at))
         total_direct = core
         kappa_bar = jnp.zeros((NZ, ROWS, COLS), F32)
         for n in range(4):
@@ -336,7 +403,7 @@
         obar[...] = kappa_bar.reshape(CHUNKS, 8, COLS) * slope[...]
 
     def pull_closure(h1_ref, h2_ref):
-        @pl.loop(0, CHUNKS)
+        @pl.loop(0, CHUNKS, unroll=CHUNKS)
         def _(chunk):
             heads = jnp.zeros((HID, COLS), F32)
             for s in range(0, 8, sub):
@@ -359,7 +426,7 @@
             acch[...] += heads
 
     def pull_features():
-        @pl.loop(0, CHUNKS)
+        @pl.loop(0, CHUNKS, unroll=CHUNKS)
         def _(chunk):
             d1 = dz1[chunk]
             d = dot(w1_bwd[...], jnp.concatenate([d1, d1[:HID]], axis=0))
@@ -367,7 +434,7 @@
                 dfeat[chunk, 8 * q : 8 * q + 8, :] = d[:8, COLS * q : COLS * (q + 1)]
 
     def add_weights(feats, h1_ref):
-        @pl.loop(0, CHUNKS)
+        @pl.loop(0, CHUNKS, unroll=CHUNKS)
         def _(chunk):
             acc2[...] += dot_nt(h1_ref[chunk], dz2[chunk])
             f = jnp.concatenate([feats[chunk, 8 * q : 8 * q + 8, :] for q in range(8)], axis=1)
@@ -400,18 +467,25 @@
         wet = (k < depth_here).astype(F32)
         wet_ext[k, 8:24, :] = wet
         wet_ext[NZ + k, 8:24, :] = wet
-    state0[:, 8:24, :] = tracers[...]
-    adj0[:, 8:24, :] = cotangent[...]
+    pack(wet_ext, send0, 16)
+    loads[0].wait()
     pack(state0, send0, 0)
+    loads[1].wait()
     pack(adj0, send0, 8)
-    pack(wet_ext, send0, 16)
 
     @pl.when(at_bottom)
     def _():
         for recvs in (recv0, recv1, recv2):
             recvs[SOUTH] = jnp.zeros(recvs.shape[1:], F32)
 
-    pl.semaphore_wait(barrier, lat_count + lon_count - 2)
+    @pl.when(jnp.logical_not(at_top))
+    def _():
+        pl.semaphore_wait(barrier, greeted)
+
+    @pl.when(at_top)
+    def _():
+        pl.semaphore_wait(barrier, greeted + lon_count - 1)
+
     start_phase(0, send0, recv0, fold0)
 
     w1_rows[0:6, :] = w_first[...]
@@ -472,37 +546,39 @@
     pull_closure(h1_0, h2_0)
     add_weights(feats0, h1_0)
 
-    piece = HID // lat_count
-    both = piece + 8
+    plane = x_count * sizes["y_high"] * y_low_count
+    pillar = core_count * sizes["z"]
+    piece, spare = piece_rows(plane)
     second = (
         (acc2[HID:, HID:] + acc2[HID:, :HID]) + acc2[:HID, HID:]
     ) + acc2[:HID, :HID]
     first = (acc1[8:, :HID] + acc1[:8, HID:]) + acc1[:8, :HID]
     head_row = jnp.sum(acch[...].T, axis=0, keepdims=True)
     extra = jnp.where(sub8 == 6, jnp.broadcast_to(head_row, (8, COLS)), first)
-    for p in range(lat_count):
+    for p in range(plane):
         parts[p, :piece, :] = second[piece * p : piece * (p + 1)]
-        parts[p, piece:, :] = extra
-
-    def lat_copy(o, src, dst, step):
-        return pltpu.make_async_remote_copy(
-            src_ref=src, dst_ref=dst, send_sem=sum_send.at[step], recv_sem=sum_recv.at[step],
-            device_id={"lat": lax.rem(lat + o, lat_count), "lon": lon}, device_id_type=MESH,
-        )
-
-    def lon_copy(o, src, dst, step):
-        return pltpu.make_async_remote_copy(
-            src_ref=src, dst_ref=dst, send_sem=sum_send.at[step], recv_sem=sum_recv.at[step],
-            device_id={"lat": lat, "lon": lax.rem(lon + o, lon_count)}, device_id_type=MESH,
-        )
+        if spare * p < 8:
+            parts[p, piece:, :] = extra[spare * p : spare * (p + 1)]
+        else:
+            parts[p, piece:, :] = jnp.zeros((spare, COLS), F32)
+
+    def share(dims, step, source, target):
+        me = slot(dims, here)
+        for offset in offsets(dims, sizes):
+            there = moved(offset)
+            pltpu.make_async_remote_copy(
+                src_ref=source(slot(dims, there)), dst_ref=target.at[me],
+                send_sem=sum_send.at[step], recv_sem=sum_recv.at[step],
+                device_id=device_at(there), device_id_type=MESH,
+            ).start()
+        return me
 
     def wait_all(ref, count, sem):
         some = ref.at[pl.ds(0, count)]
         pltpu.make_async_copy(some, some, sem).wait()
 
-    for o in range(1, lat_count):
-        lat_copy(o, parts.at[lax.rem(lat + o, lat_count)], parts_lat.at[lat], 0).start()
-    parts_lat[lat] = parts[lat]
+    me = share(PLANE, 0, lambda there: parts.at[there], parts_plane)
+    parts_plane[me] = parts[me]
 
     pull_features()
 
@@ -511,34 +587,40 @@
 
     pull_state(finish)
 
-    wait_all(parts_lat, lat_count - 1, sum_recv.at[0])
-    summed = parts_lat[0]
-    for p in range(1, lat_count):
-        summed = summed + parts_lat[p]
-    parts_lon[lon] = summed
-    for o in range(1, lon_count):
-        lon_copy(o, parts_lon.at[lon], parts_lon.at[lon], 1).start()
-    wait_all(parts_lon, lon_count - 1, sum_recv.at[1])
-    summed = parts_lon[0]
-    for p in range(1, lon_count):
-        summed = summed + parts_lon[p]
+    wait_all(parts_plane, plane - 1, sum_recv.at[0])
+    summed = parts_plane[0]
+    for p in range(1, plane):
+        summed = summed + parts_plane[p]
+    me = slot(PILLAR, here)
+    parts_pillar[me] = summed
+    share(PILLAR, 1, lambda there: parts_pillar.at[me], parts_pillar)
+    wait_all(parts_pillar, pillar - 1, sum_recv.at[1])
+    summed = parts_pillar[0]
+    for p in range(1, pillar):
+        summed = summed + parts_pillar[p]
     cells_all = lat_count * ROWS * lon_count * COLS * NZ
-    summed = summed * (1.0 / math.sqrt(cells_all))
-    gathered[lat] = summed[:piece]
-    for o in range(1, lat_count):
-        lat_copy(o, gathered.at[lat], gathered.at[lat], 2).start()
-    gw_first[...] = summed[piece : piece + 6]
-    gw_head[...] = summed[piece + 6 : piece + 7]
-    wait_all(gathered, lat_count - 1, sum_recv.at[2])
-    for p in range(lat_count):
-        gw_second[piece * p : piece * (p + 1), :] = gathered[p]
+    me = slot(PLANE, here)
+    gathered[me] = summed * (1.0 / math.sqrt(cells_all))
+    share(PLANE, 2, lambda there: gathered.at[me], gathered)
+    wait_all(gathered, plane - 1, sum_recv.at[2])
+    for p in range(plane):
+        gw_second[piece * p : piece * (p + 1), :] = gathered[p, :piece, :]
+        if spare * p < 8:
+            extras[spare * p : spare * (p + 1), :] = gathered[p, piece:, :]
+    gw_first[...] = extras[0:6, :]
+    gw_head[...] = extras[6:7, :]
 
     finish_phase(0, send0, recv0, fold0)
     finish_phase(1, send1, recv1, fold1)
     finish_phase(2, send2, recv2, fold2)
-    wait_all(parts_lat, lat_count - 1, sum_send.at[0])
-    wait_all(parts_lon, lon_count - 1, sum_send.at[1])
-    wait_all(gathered, lat_count - 1, sum_send.at[2])
+    wait_all(parts_plane, plane - 1, sum_send.at[0])
+    wait_all(parts_pillar, pillar - 1, sum_send.at[1])
+    wait_all(gathered, plane - 1, sum_send.at[2])
+
+
+def hand_over(*refs):
+    for source, target in zip(refs[:5], refs[5:]):
+        target[...] = source[...]
 
 
 def per_device(lat_count, lon_count, sub, tracers, land_mask, level_counts, fold_partner, cotangent,
@@ -550,8 +632,10 @@
     stack = pltpu.VMEM((CHUNKS, 2 * HID, LANES), BF16)
     dense = pltpu.VMEM((CHUNKS, HID, LANES), F32)
     tile = pltpu.VMEM((CHUNKS, 8, COLS), F32)
-    piece = HID // lat_count
-    both = piece + 8
+    sizes = place_sizes(lat_count, lon_count)
+    plane = sizes["x"] * sizes["y_low"] * sizes["y_high"]
+    pillar = sizes["core"] * sizes["z"]
+    both = sum(piece_rows(plane))
     scratch = [
         pltpu.VMEM((8, HID), F32),
         pltpu.VMEM((HID, 32), BF16),
@@ -581,19 +665,21 @@
     scratch += [pltpu.VMEM((4, n, COLS), F32) for n in (24, 8, 8)] * 2
     scratch += [pltpu.VMEM((lon_count, n, COLS), F32) for n in (24, 8, 8)]
     scratch += [
-        pltpu.VMEM((lat_count, both, COLS), F32),
-        pltpu.VMEM((lat_count, both, COLS), F32),
-        pltpu.VMEM((lon_count, both, COLS), F32),
+        pltpu.VMEM((plane, both, COLS), F32),
+        pltpu.VMEM((plane, both, COLS), F32),
+        pltpu.VMEM((pillar, both, COLS), F32),
+        pltpu.VMEM((plane, both, COLS), F32),
         pltpu.VMEM((8, COLS), F32),
-        pltpu.VMEM((lat_count, piece, COLS), F32),
         pltpu.SemaphoreType.DMA((3, 4)),
         pltpu.SemaphoreType.DMA((3, 4)),
         pltpu.SemaphoreType.DMA((3,)),
         pltpu.SemaphoreType.DMA((3,)),
         pltpu.SemaphoreType.DMA((3,)),
         pltpu.SemaphoreType.DMA((3,)),
+        pltpu.SemaphoreType.DMA((2,)),
     ]
     vmem = pl.BlockSpec(memory_space=pltpu.VMEM)
+    anywhere = pl.BlockSpec(memory_space=pl.ANY)
     run = pl.pallas_call(
         lambda *refs: kernel(lat_count, lon_count, sub, *refs),
         out_shape=[
@@ -603,7 +689,8 @@
             jax.ShapeDtypeStruct((HID, HID), F32),
             jax.ShapeDtypeStruct((1, HID), F32),
         ],
-        in_specs=[vmem] * 10 + [pl.BlockSpec(memory_space=pltpu.SMEM)],
+        in_specs=[anywhere] + [vmem] * 3 + [anywhere] + [vmem] * 5
+        + [pl.BlockSpec(memory_space=pltpu.SMEM)],
         out_specs=[vmem] * 5,
         scratch_shapes=scratch,
         compiler_params=pltpu.CompilerParams(
@@ -611,11 +698,18 @@
         ),
         name="adjoint_steps",
     )
-    out, grad, first, second, head = run(
+    results = run(
         tracers.reshape(field), land_mask, level_counts, fold_partner.reshape(1, COLS),
         cotangent.reshape(field), w_first, b_first.reshape(1, HID), w_second,
         b_second.reshape(1, HID), w_head.reshape(1, HID), b_head,
     )
+    out, grad, first, second, head = pl.pallas_call(
+        hand_over,
+        out_shape=[jax.ShapeDtypeStruct(r.shape, F32) for r in results],
+        in_specs=[vmem] * 5,
+        out_specs=[vmem] * 5,
+        name="hand_over",
+    )(*results)
     return (
         out.reshape(tracers.shape), grad.reshape(tracers.shape), first, second, head.reshape(HID)
     )
@@ -625,7 +719,7 @@
     lat_count, lon_count = mesh.shape["lat"], mesh.shape["lon"]
     grid = P(None, None, "lat", "lon")
     return jax.shard_map(
-        lambda *args: per_device(lat_count, lon_count, 2, *args),
+        lambda *args: per_device(lat_count, lon_count, 8, *args),
         mesh=mesh,
         in_specs=(
             grid, P("lat", "lon"), P("lat", "lon"), P("lon"), grid,

time: 64.1 us -> 53.9 us (0.84)
  Pallas kernels: 58.7 us -> 52.3 us
  local copies, waits for them, and re-layouts: 3.93 us -> 0 us
    pallas_call x1, Pallas kernels: 58.7 us -> 50.8 us  [per_device(): run(tracers.reshape(field), land_mask, level_counts, fold_partner.reshape...]
    unnamed x13 -> x0, local copies, waits for them, and re-layouts: 3.93 us -> none
    pallas_call x0 -> x1, Pallas kernels: none -> 1.59 us  [per_device(): pl.pallas_call(hand_over, out_shape=[jax.ShapeDtypeStruct(r.shape, F32) f...]
where the time goes in v2:
time: 53.9 us; the launch traced here: 53.6 us
  Pallas kernels  52.3 us (97%)
  between operations  1.29 us (2%)
    pallas_call x1, Pallas kernels, per_device(): run(tracers.reshape(field), land_mask, level_counts, fold_partner.reshape...  50.8 us
    pallas_call x1, Pallas kernels, per_device(): pl.pallas_call(hand_over, out_shape=[jax.ShapeDtypeStruct(r.shape, F32) f...  1.59 us

profile of v2, /device:TPU:1, one launch (start us, length us, event | category | flops | bytes accessed | tf_op | source)
XLA Modules:
  0.0 53.6 jit_solution(11710491635190044468)
XLA Ops:
  1.3 50.8 %adjoint_steps.1 = (f32[8,16,128]{2,1,0:T(8,128)}, f32[8,16,128]{2,1,0:T(8,128)}, f32[6,128]{1,0:T(8,128)}, f32[128,128]{1,0:T(8,128)}, f32[1,128]{1,0:T(1,128)}) custom-call(f32[8,16,128]{2,1,0:T(8,128)} %bitcast.9, s32[16,128]{1,0:T(8,128)} %refs_1_.1, s32[16,128]{1,0:T(8,128)} %refs_2_.1, s32[1,128]{1,0:T(1,128)} %bitcast.11, f32[8,16,128]{2,1,0:T(8,128)} %bitcast.10, ...), custom_call_target="tpu_custom_call" | custom-call | tf_op jit(solution)/shard_map/adjoint_steps/pallas_call | solution.py:701
  52.0 1.6 %hand_over.1 = (f32[8,16,128]{2,1,0:T(8,128)}, f32[8,16,128]{2,1,0:T(8,128)}, f32[6,128]{1,0:T(8,128)}, f32[128,128]{1,0:T(8,128)}, f32[1,128]{1,0:T(1,128)}) custom-call(f32[8,16,128]{2,1,0:T(8,128)} %get-tuple-element.15.refs_0_, f32[8,16,128]{2,1,0:T(8,128)} %get-tuple-element.16.refs_1_, f32[6,128]{1,0:T(8,128)} %get-tuple-element.17.refs_2_, ...), custom_call_target="tpu_custom_call" | custom-call | tf_op jit(solution)/shard_map/hand_over/pallas_call | solution.py:706

commit v3 on v2

--- a/solution.py
+++ b/solution.py
@@ -20,11 +20,13 @@
 CHUNKS = NZ * ROWS // 8
 LANES = 8 * COLS
 EAST, WEST, NORTH, SOUTH = 0, 1, 2, 3
+HALF = NZ * ROWS
 OPPOSITE = (WEST, EAST, SOUTH, NORTH)
 
 
 PLANE = ("x", "y_high", "y_low")
 PILLAR = ("core", "z")
+RIM = ("z", "y_low")
 
 
 def place_sizes(lat_count, lon_count):
@@ -73,12 +75,13 @@
 
 
 def kernel(
-    lat_count, lon_count, sub,
+    lat_count, lon_count,
     tracers, land, levels, partner, cotangent, w_first, b_first, w_second, b_second, w_head, b_head,
     tracers_out, tracer_grad, gw_first, gw_second, gw_head,
     w1_rows, w1_fwd, w1_bwd, w2_fwd, w2_bwd, bias2, head,
     wet_ext, pair, state0, state1, adj0, adj1, kap0, kap1, contrast0, contrast1, coef0, coef1,
-    slope0, slope1, direct, feats0, feats1, logits, h1_0, h1_1, h2_0, h2_1, dz2, dz1, dfeat,
+    slope0, slope1, direct, feats0, feats1, logits, h1_0, h1_1, h2_0, h2_1, dz2, dz1,
+    h1_edge, h2_edge, dfeat,
     obar, acc2, acc1, acch,
     send0, send1, send2, recv0, recv1, recv2, fold0, fold1, fold2,
     parts, parts_plane, parts_pillar, gathered, extras,
@@ -121,20 +124,20 @@
     def greet(device):
         pl.semaphore_signal(barrier, inc=1, device_id=device, device_id_type=MESH)
 
+    @pl.when(at_top)
+    def _():
+        for offset in offsets(RIM, sizes):
+            greet(device_at(moved(offset)))
+
     greeted = 4
+    for dims in (PILLAR, PLANE):
+        for offset in offsets(dims, sizes):
+            greet(device_at(moved(offset)))
+            greeted += 1
     greet({"lat": lat, "lon": east})
     greet({"lat": lat, "lon": west})
     greet({"lat": lax.rem(lat + 1, lat_count), "lon": lon})
     greet({"lat": lax.rem(lat + lat_count - 1, lat_count), "lon": lon})
-    for dims in (PLANE, PILLAR):
-        for offset in offsets(dims, sizes):
-            greet(device_at(moved(offset)))
-            greeted += 1
-
-    @pl.when(at_top)
-    def _():
-        for o in range(1, lon_count):
-            greet({"lat": lat, "lon": lax.rem(lon + o, lon_count)})
 
     loads = [
         pltpu.make_async_copy(tracers, state0.at[:, pl.ds(8, ROWS), :], in_sem.at[0]),
@@ -162,26 +165,28 @@
         )
 
     def start_phase(phase, sends, recvs, folds):
-        to_side(phase, EAST, sends, recvs).start()
-        to_side(phase, WEST, sends, recvs).start()
-
-        @pl.when(jnp.logical_not(at_top))
-        def _():
-            to_side(phase, NORTH, sends, recvs).start()
-
-        @pl.when(jnp.logical_not(at_bottom))
-        def _():
-            to_side(phase, SOUTH, sends, recvs).start()
-
         @pl.when(at_top)
         def _():
-            for o in range(1, lon_count):
+            for offset in offsets(RIM, sizes):
                 pltpu.make_async_remote_copy(
                     src_ref=sends.at[NORTH], dst_ref=folds.at[lon],
                     send_sem=fold_send.at[phase], recv_sem=fold_recv.at[phase],
-                    device_id={"lat": lat, "lon": lax.rem(lon + o, lon_count)},
-                    device_id_type=MESH,
+                    device_id=device_at(moved(offset)), device_id_type=MESH,
                 ).start()
+
+        to_side(phase, EAST, sends, recvs).start()
+        to_side(phase, WEST, sends, recvs).start()
+
+        @pl.when(jnp.logical_not(at_top))
+        def _():
+            to_side(phase, NORTH, sends, recvs).start()
+
+        @pl.when(jnp.logical_not(at_bottom))
+        def _():
+            to_side(phase, SOUTH, sends, recvs).start()
+
+        @pl.when(at_top)
+        def _():
             folds[lon] = sends[NORTH]
 
     def wait_phase(phase, sends, recvs, folds):
@@ -289,53 +294,60 @@
             store_feature(feats, CHUNKS, t, cells)
             store_feature(feats, CHUNKS, 2 + t, -pltpu.roll(vertical, 1, 0))
             store_feature(feats, CHUNKS, 4 + t, vertical)
-        east_row = jnp.broadcast_to(recvs[EAST, 0:1, :], (8, COLS))
-        west_row = jnp.broadcast_to(recvs[WEST, 7:8, :], (8, COLS))
-        first = lane8 < NZ * ROWS
-        wet_col = edge_wet()
-        joint = jnp.where(
-            lax.rem(lane8, NZ * ROWS) >= (NZ - 1) * ROWS, 0.0,
-            wet_col * pltpu.roll(wet_col, COLS - ROWS, 1),
+        column_features(
+            recvs[EAST, 0:1, :], recvs[WEST, 7:8, :], edge_wet(), feats, CHUNKS + 1
         )
-        fields = (
-            jnp.where(first, east_row, pltpu.roll(west_row, NZ * ROWS, 1)),
-            jnp.where(first, pltpu.roll(east_row, NZ * ROWS, 1), west_row),
+        return wet
+
+    def paired(east_row, west_row):
+        east_row = jnp.broadcast_to(east_row, (8, COLS))
+        west_row = jnp.broadcast_to(west_row, (8, COLS))
+        first = lane8 < HALF
+        return (
+            jnp.where(first, east_row, pltpu.roll(west_row, HALF, 1)),
+            jnp.where(first, pltpu.roll(east_row, HALF, 1), west_row),
         )
-        for t, cells in enumerate(fields):
+
+    def joint_column(wet_col):
+        below = pltpu.roll(wet_col, COLS - ROWS, 1)
+        return jnp.where(lax.rem(lane8, HALF) >= HALF - ROWS, 0.0, wet_col * below)
+
+    def column_features(east_row, west_row, wet_col, feats, chunk):
+        joint = joint_column(wet_col)
+        for t, cells in enumerate(paired(east_row, west_row)):
             vertical = (pltpu.roll(cells, COLS - ROWS, 1) - cells) * joint
-            feats[CHUNKS + 1, t : t + 1, :] = cells[0:1]
-            feats[CHUNKS + 1, 2 + t : 3 + t, :] = -pltpu.roll(vertical, ROWS, 1)[0:1]
-            feats[CHUNKS + 1, 4 + t : 5 + t, :] = vertical[0:1]
-        return wet
+            feats[chunk, t : t + 1, :] = cells[0:1]
+            feats[chunk, 2 + t : 3 + t, :] = -pltpu.roll(vertical, ROWS, 1)[0:1]
+            feats[chunk, 4 + t : 5 + t, :] = vertical[0:1]
 
     def edge_wet():
-        wet_east = jnp.broadcast_to(recv0[EAST, 16:17, :], (8, COLS))
-        wet_west = jnp.broadcast_to(recv0[WEST, 23:24, :], (8, COLS))
-        return jnp.where(lane8 < NZ * ROWS, wet_east, wet_west)
+        return paired(recv0[EAST, 16:17, :], recv0[WEST, 23:24, :])[0]
+
+    def own_edge_wet():
+        return paired(send0[EAST, 23:24, :], send0[WEST, 16:17, :])[0]
 
     def wide(x, n):
         return jnp.concatenate([x] * n, axis=1) if n > 1 else x
 
-    def closure_chunk(feats, chunk, rows, h1_ref, h2_ref):
-        for s in range(0, rows, sub):
-            n = min(sub, rows - s)
-            f = [feats[chunk, 8 * (s + q) : 8 * (s + q) + 8, :] for q in range(n)]
-            f = jnp.concatenate(f, axis=1) if n > 1 else f[0]
-            high = f.astype(BF16).astype(F32)
-            low = f - high
-            stacked = jnp.concatenate([high, low, high, low], axis=0).astype(BF16)
-            h1 = jnp.tanh(dot(w1_fwd[...], stacked))
-            h1_high, h1_low = halves(h1)
-            pre2 = dot(w2_fwd[...], jnp.concatenate([h1_high, h1_low, h1_high], axis=0))
-            h2 = jnp.tanh(pre2 + wide(bias2[...], n))
-            o = jnp.sum(h2 * wide(head[...], n), axis=0, keepdims=True)
-            for q in range(n):
-                logits[chunk, s + q : s + q + 1, :] = o[:, COLS * q : COLS * (q + 1)]
-            if h1_ref is not None:
-                lanes = slice(COLS * s, COLS * (s + n))
-                h1_ref[chunk, :HID, lanes] = h1_high
-                h1_ref[chunk, HID:, lanes] = h1_low
-                h2_ref[chunk, :, lanes] = h2
+    def closure_chunk(feats, chunk, rows, h1_ref, h2_ref, at=None):
+        at = chunk if at is None else at
+        n = rows
+        f = [feats[chunk, 8 * q : 8 * q + 8, :] for q in range(n)]
+        f = jnp.concatenate(f, axis=1) if n > 1 else f[0]
+        high = f.astype(BF16).astype(F32)
+        low = f - high
+        stacked = jnp.concatenate([high, low, high, low], axis=0).astype(BF16)
+        h1 = jnp.tanh(dot(w1_fwd[...], stacked))
+        h1_high, h1_low = halves(h1)
+        pre2 = dot(w2_fwd[...], jnp.concatenate([h1_high, h1_low, h1_high], axis=0))
+        h2 = jnp.tanh(pre2 + wide(bias2[...], n))
+        o = jnp.sum(h2 * wide(head[...], n), axis=0, keepdims=True)
+        for q in range(n):
+            logits[chunk, q : q + 1, :] = o[:, COLS * q : COLS * (q + 1)]
+        if h1_ref is not None:
+            h1_ref[at, :HID, :] = h1_high
+            h1_ref[at, HID:, :] = h1_low
+            h2_ref[at] = h2
 
     def closure_own(feats, h1_ref, h2_ref):
         @pl.loop(0, CHUNKS, unroll=CHUNKS)
@@ -349,6 +361,11 @@
     def advance(phase, state, feats, sends, recvs, folds, h1_ref, h2_ref, kap, slope, contrast, coef):
         own_features(state, feats)
         closure_own(feats, h1_ref, h2_ref)
+        if phase == 1:
+            column_features(
+                sends[EAST, 7:8, :], sends[WEST, 0:1, :], own_edge_wet(), feats, CHUNKS + 2
+            )
+            closure_chunk(feats, CHUNKS + 2, 1, h1_edge, h2_edge, 0)
         wait_phase(phase, sends, recvs, folds)
         unpack(state, recvs, 0)
         if phase == 0:
@@ -402,28 +419,76 @@
         direct[...] = total_direct
         obar[...] = kappa_bar.reshape(CHUNKS, 8, COLS) * slope[...]
 
+    def pull_cells(bar, h1_high, h1_low, h2):
+        n = bar.shape[1] // COLS
+        weighted = h2 * bar
+        d2_high, d2_low = halves(wide(head[...], n) * (bar - weighted * h2))
+        dh1 = dot(w2_bwd[...], jnp.concatenate([d2_high, d2_low, d2_high], axis=0))
+        h1 = h1_high.astype(F32) + h1_low.astype(F32)
+        d1_high, d1_low = halves(dh1 * (1.0 - h1 * h1))
+        return weighted, d2_high, d2_low, d1_high, d1_low
+
     def pull_closure(h1_ref, h2_ref):
         @pl.loop(0, CHUNKS, unroll=CHUNKS)
         def _(chunk):
-            heads = jnp.zeros((HID, COLS), F32)
-            for s in range(0, 8, sub):
-                n = min(sub, 8 - s)
-                lanes = slice(COLS * s, COLS * (s + n))
-                bar = [obar[chunk, s + q : s + q + 1, :] for q in range(n)]
-                bar = jnp.concatenate(bar, axis=1) if n > 1 else bar[0]
-                h2 = h2_ref[chunk, :, lanes]
-                weighted = h2 * bar
-                for q in range(n):
-                    heads = heads + weighted[:, COLS * q : COLS * (q + 1)]
-                d2_high, d2_low = halves(wide(head[...], n) * (bar - weighted * h2))
-                dh1 = dot(w2_bwd[...], jnp.concatenate([d2_high, d2_low, d2_high], axis=0))
-                h1 = h1_ref[chunk, :HID, lanes].astype(F32) + h1_ref[chunk, HID:, lanes].astype(F32)
-                d1_high, d1_low = halves(dh1 * (1.0 - h1 * h1))
-                dz2[chunk, :HID, lanes] = d2_high
-                dz2[chunk, HID:, lanes] = d2_low
-                dz1[chunk, :HID, lanes] = d1_high
-                dz1[chunk, HID:, lanes] = d1_low
+            bar = jnp.concatenate([obar[chunk, q : q + 1, :] for q in range(8)], axis=1)
+            weighted, d2_high, d2_low, d1_high, d1_low = pull_cells(
+                bar, h1_ref[chunk, :HID, :], h1_ref[chunk, HID:, :], h2_ref[chunk]
+            )
+            dz2[chunk, :HID, :] = d2_high
+            dz2[chunk, HID:, :] = d2_low
+            dz1[chunk, :HID, :] = d1_high
+            dz1[chunk, HID:, :] = d1_low
+            heads = weighted[:, :COLS]
+            for q in range(1, 8):
+                heads = heads + weighted[:, COLS * q : COLS * (q + 1)]
             acch[...] += heads
+
+    def send_edges(h1_ref, h2_ref, sends):
+        tops = [(2 * k + 1, 7) for k in range(NZ)]
+        lows = [(2 * k, 0) for k in range(NZ)]
+        places = tops + lows
+        turned = jnp.concatenate(
+            [obar[...].reshape(HALF, COLS), jnp.zeros((HALF, COLS), F32)], axis=0
+        ).T
+        column_bar = paired(turned[COLS - 1 :], turned[0:1])[0][0:1]
+        bar = jnp.concatenate([obar[c, q : q + 1, :] for c, q in places] + [column_bar], axis=1)
+        cut = [slice(COLS * q, COLS * (q + 1)) for _, q in places]
+        high = [h1_ref[c, :HID, l] for (c, _), l in zip(places, cut)] + [h1_edge[0, :HID, :]]
+        low = [h1_ref[c, HID:, l] for (c, _), l in zip(places, cut)] + [h1_edge[0, HID:, :]]
+        h2 = [h2_ref[c, :, l] for (c, _), l in zip(places, cut)] + [h2_edge[0]]
+        high, low, h2 = (jnp.concatenate(x, axis=1) for x in (high, low, h2))
+        _, _, _, d1_high, d1_low = pull_cells(bar, high, low, h2)
+        d = dot(w1_bwd[...], jnp.concatenate([d1_high, d1_low, d1_high], axis=0))
+        d = [d[:8, COLS * i : COLS * (i + 1)] for i in range(len(places) + 1)]
+        for side, y in ((NORTH, ROWS - 1), (SOUTH, 0)):
+            rows = d[:NZ] if side == NORTH else d[NZ : 2 * NZ]
+            wets = [wet_ext[k, 8 + y : 9 + y, :] for k in range(NZ)]
+            vertical = [
+                (pltpu.roll(rows[k], 4, 0) - pltpu.roll(rows[k + 1], 6, 0))
+                * (wets[k + 1] * wets[k])
+                for k in range(NZ - 1)
+            ]
+            for k in range(NZ):
+                value = rows[k]
+                if k < NZ - 1:
+                    value = value - vertical[k]
+                if k > 0:
+                    value = value + vertical[k - 1]
+                for t in range(2):
+                    i = NZ * t + k
+                    sends[side, i : i + 1, :] = value[t : t + 1] + direct[i, y : y + 1, :]
+        cells = d[2 * NZ]
+        vertical = pltpu.roll(cells, 4, 0) - pltpu.roll(pltpu.roll(cells, 6, 0), COLS - ROWS, 1)
+        vertical = vertical * joint_column(own_edge_wet())
+        value = cells - vertical + pltpu.roll(vertical, ROWS, 1)
+        other = pltpu.roll(value, HALF, 1)
+        first = lane8[0:1] < HALF
+        turned = direct[...].reshape(COLS, COLS).T
+        from_east = turned[COLS - 1 :] + jnp.where(first, value[0:1], other[1:2])
+        from_west = turned[0:1] + jnp.where(first, other[0:1], value[1:2])
+        sends[EAST] = jnp.broadcast_to(from_east, (8, COLS))
+        sends[WEST] = jnp.broadcast_to(from_west, (8, COLS))
 
     def pull_features():
         @pl.loop(0, CHUNKS, unroll=CHUNKS)
@@ -515,6 +580,7 @@
             feats[chunk, pl.ds(6, 8, stride=8), :] = jnp.ones((8, COLS), F32)
             feats[chunk, pl.ds(7, 8, stride=8), :] = jnp.zeros((8, COLS), F32)
         feats[CHUNKS + 1, 0:8, :] = ones_row
+        feats[CHUNKS + 2, 0:8, :] = ones_row
     logits[CHUNKS + 1] = jnp.zeros((8, COLS), F32)
     acc2[...] = jnp.zeros_like(acc2)
     acc1[...] = jnp.zeros_like(acc1)
@@ -530,6 +596,8 @@
     )
 
     pull_flux(adj0, recv0, 8, contrast1, coef1, slope1)
+    send_edges(h1_1, h2_1, send2)
+    start_phase(2, send2, recv2, fold2)
     pull_closure(h1_1, h2_1)
     pull_features()
 
@@ -537,8 +605,6 @@
         adj1[i, 8 + 8 * half : 16 + 8 * half, :] = value
 
     pull_state(keep)
-    pack(adj1, send2, 0)
-    start_phase(2, send2, recv2, fold2)
     add_weights(feats1, h1_1)
     wait_phase(2, send2, recv2, fold2)
     unpack(adj1, recv2, 0)
@@ -623,12 +689,12 @@
         target[...] = source[...]
 
 
-def per_device(lat_count, lon_count, sub, tracers, land_mask, level_counts, fold_partner, cotangent,
+def per_device(lat_count, lon_count, tracers, land_mask, level_counts, fold_partner, cotangent,
                w_first, b_first, w_second, b_second, w_head, b_head):
     field = (FIELDS, ROWS, COLS)
     ext = pltpu.VMEM((FIELDS, 32, COLS), F32)
     kap = pltpu.VMEM((NZ, 32, COLS), F32)
-    feats = pltpu.VMEM((CHUNKS + 2, 64, COLS), F32)
+    feats = pltpu.VMEM((CHUNKS + 3, 64, COLS), F32)
     stack = pltpu.VMEM((CHUNKS, 2 * HID, LANES), BF16)
     dense = pltpu.VMEM((CHUNKS, HID, LANES), F32)
     tile = pltpu.VMEM((CHUNKS, 8, COLS), F32)
@@ -654,8 +720,10 @@
         tile, tile,
         pltpu.VMEM(field, F32),
         feats, feats,
-        pltpu.VMEM((CHUNKS + 2, 8, COLS), F32),
+        pltpu.VMEM((CHUNKS + 3, 8, COLS), F32),
         stack, stack, dense, dense, stack, stack,
+        pltpu.VMEM((1, 2 * HID, COLS), BF16),
+        pltpu.VMEM((1, HID, COLS), F32),
         pltpu.VMEM((CHUNKS, 64, COLS), F32),
         tile,
         pltpu.VMEM((2 * HID, 2 * HID), F32),
@@ -681,7 +749,7 @@
     vmem = pl.BlockSpec(memory_space=pltpu.VMEM)
     anywhere = pl.BlockSpec(memory_space=pl.ANY)
     run = pl.pallas_call(
-        lambda *refs: kernel(lat_count, lon_count, sub, *refs),
+        lambda *refs: kernel(lat_count, lon_count, *refs),
         out_shape=[
             jax.ShapeDtypeStruct(field, F32),
             jax.ShapeDtypeStruct(field, F32),
@@ -719,7 +787,7 @@
     lat_count, lon_count = mesh.shape["lat"], mesh.shape["lon"]
     grid = P(None, None, "lat", "lon")
     return jax.shard_map(
-        lambda *args: per_device(lat_count, lon_count, 8, *args),
+        lambda *args: per_device(lat_count, lon_count, *args),
         mesh=mesh,
         in_specs=(
             grid, P("lat", "lon"), P("lat", "lon"), P("lon"), grid,

time: 53.9 us -> 50.7 us (0.941)
  Pallas kernels: 52.3 us -> 49.1 us
    pallas_call x1, Pallas kernels: 50.8 us -> 47.6 us  [per_device(): run(tracers.reshape(field), land_mask, level_counts, fold_partner.reshape...]
where the time goes in v3:
time: 50.7 us; the launch traced here: 50.4 us
  Pallas kernels  49.1 us (97%)
  between operations  1.29 us (3%)
    pallas_call x1, Pallas kernels, per_device(): run(tracers.reshape(field), land_mask, level_counts, fold_partner.reshape...  47.6 us
    pallas_call x1, Pallas kernels, per_device(): pl.pallas_call(hand_over, out_shape=[jax.ShapeDtypeStruct(r.shape, F32) f...  1.59 us

profile of v3, /device:TPU:1, one launch (start us, length us, event | category | flops | bytes accessed | tf_op | source)
XLA Modules:
  0.0 50.4 jit_solution(12231146820483549313)
XLA Ops:
  1.3 47.6 %adjoint_steps.1 = (f32[8,16,128]{2,1,0:T(8,128)}, f32[8,16,128]{2,1,0:T(8,128)}, f32[6,128]{1,0:T(8,128)}, f32[128,128]{1,0:T(8,128)}, f32[1,128]{1,0:T(1,128)}) custom-call(f32[8,16,128]{2,1,0:T(8,128)} %bitcast.9, s32[16,128]{1,0:T(8,128)} %refs_1_.1, s32[16,128]{1,0:T(8,128)} %refs_2_.1, s32[1,128]{1,0:T(1,128)} %bitcast.11, f32[8,16,128]{2,1,0:T(8,128)} %bitcast.10, ...), custom_call_target="tpu_custom_call" | custom-call | tf_op jit(solution)/shard_map/adjoint_steps/pallas_call | solution.py:769
  48.8 1.6 %hand_over.1 = (f32[8,16,128]{2,1,0:T(8,128)}, f32[8,16,128]{2,1,0:T(8,128)}, f32[6,128]{1,0:T(8,128)}, f32[128,128]{1,0:T(8,128)}, f32[1,128]{1,0:T(1,128)}) custom-call(f32[8,16,128]{2,1,0:T(8,128)} %get-tuple-element.15.refs_0_, f32[8,16,128]{2,1,0:T(8,128)} %get-tuple-element.16.refs_1_, f32[6,128]{1,0:T(8,128)} %get-tuple-element.17.refs_2_, ...), custom_call_target="tpu_custom_call" | custom-call | tf_op jit(solution)/shard_map/hand_over/pallas_call | solution.py:774

commit v4 on v3

--- a/solution.py
+++ b/solution.py
@@ -83,9 +83,11 @@
     slope0, slope1, direct, feats0, feats1, logits, h1_0, h1_1, h2_0, h2_1, dz2, dz1,
     h1_edge, h2_edge, dfeat,
     obar, acc2, acc1, acch,
-    send0, send1, send2, recv0, recv1, recv2, fold0, fold1, fold2,
+    beside_out, beside_in, across_out, across_in, wet_beside_out, wet_beside_in, first_out, first_in,
+    fold_first, folded,
     parts, parts_plane, parts_pillar, gathered, extras,
     send_sem, recv_sem, fold_send, fold_recv, sum_send, sum_recv, in_sem,
+    land_here, levels_here, partner_here, w1_here, b1_here, w2_here, b2_here, wh_here,
 ):
     lat = lax.axis_index("lat")
     lon = lax.axis_index("lon")
@@ -119,6 +121,23 @@
             index = index * sizes[d] + at[d]
         return index
 
+    def load(i, source, target):
+        copy = pltpu.make_async_copy(source, target, in_sem.at[i])
+        copy.start()
+        return copy
+
+    loads = [
+        load(0, land, land_here),
+        load(1, levels, levels_here),
+        load(2, tracers, state0.at[:, pl.ds(8, ROWS), :]),
+        load(3, cotangent, adj0.at[:, pl.ds(8, ROWS), :]),
+        load(4, partner, partner_here),
+        load(5, w_first, w1_here),
+        load(6, b_first, b1_here),
+        load(7, w_second, w2_here),
+        load(8, b_second, b2_here),
+        load(9, w_head, wh_here),
+    ]
     barrier = pltpu.get_barrier_semaphore()
 
     def greet(device):
@@ -139,16 +158,25 @@
     greet({"lat": lax.rem(lat + 1, lat_count), "lon": lon})
     greet({"lat": lax.rem(lat + lat_count - 1, lat_count), "lon": lon})
 
-    loads = [
-        pltpu.make_async_copy(tracers, state0.at[:, pl.ds(8, ROWS), :], in_sem.at[0]),
-        pltpu.make_async_copy(cotangent, adj0.at[:, pl.ds(8, ROWS), :], in_sem.at[1]),
-    ]
-    for load in loads:
-        load.start()
-
     lane3 = lax.broadcasted_iota(jnp.int32, (FIELDS, ROWS, COLS), 2)
     lane8 = lax.broadcasted_iota(jnp.int32, (8, COLS), 1)
     sub8 = lax.broadcasted_iota(jnp.int32, (8, COLS), 0)
+
+    send0 = {EAST: wet_beside_out.at[0], WEST: wet_beside_out.at[1],
+             NORTH: first_out.at[0], SOUTH: first_out.at[1]}
+    recv0 = {EAST: wet_beside_in.at[0], WEST: wet_beside_in.at[1],
+             NORTH: first_in.at[0], SOUTH: first_in.at[1]}
+    send1, send2, send3 = (
+        {EAST: beside_out.at[i, 0], WEST: beside_out.at[i, 1],
+         NORTH: across_out.at[i, 0], SOUTH: across_out.at[i, 1]}
+        for i in range(3)
+    )
+    recv1, recv2, recv3 = (
+        {EAST: beside_in.at[i, 0], WEST: beside_in.at[i, 1],
+         NORTH: across_in.at[i, 0], SOUTH: across_in.at[i, 1]}
+        for i in range(3)
+    )
+    fold0, fold1, fold2, fold3 = fold_first, folded.at[0], folded.at[1], folded.at[2]
 
     def to_side(phase, side, sends, recvs):
         target = {
@@ -159,7 +187,7 @@
         }[side]
         back = OPPOSITE[side]
         return pltpu.make_async_remote_copy(
-            src_ref=sends.at[side], dst_ref=recvs.at[back],
+            src_ref=sends[side], dst_ref=recvs[back],
             send_sem=send_sem.at[phase, side], recv_sem=recv_sem.at[phase, back],
             device_id=target, device_id_type=MESH,
         )
@@ -169,7 +197,7 @@
         def _():
             for offset in offsets(RIM, sizes):
                 pltpu.make_async_remote_copy(
-                    src_ref=sends.at[NORTH], dst_ref=folds.at[lon],
+                    src_ref=sends[NORTH], dst_ref=folds.at[lon],
                     send_sem=fold_send.at[phase], recv_sem=fold_recv.at[phase],
                     device_id=device_at(moved(offset)), device_id_type=MESH,
                 ).start()
@@ -187,7 +215,7 @@
 
         @pl.when(at_top)
         def _():
-            folds[lon] = sends[NORTH]
+            folds[lon] = sends[NORTH][...]
 
     def wait_phase(phase, sends, recvs, folds):
         to_side(phase, WEST, sends, recvs).wait_recv()
@@ -205,15 +233,20 @@
         def _():
             others = folds.at[pl.ds(0, lon_count - 1)]
             pltpu.make_async_copy(others, others, fold_recv.at[phase]).wait()
-            block = jnp.broadcast_to(partner[...] >> 7, (8, COLS))
-            lane = jnp.broadcast_to(partner[...] & (COLS - 1), (8, COLS))
-            for g in range(sends.shape[1] // 8):
-                rows = pl.ds(8 * g, 8)
+            block = jnp.broadcast_to(partner_here[...] >> 7, (8, COLS))
+            lane = jnp.broadcast_to(partner_here[...] & (COLS - 1), (8, COLS))
+            picked = jnp.zeros((8, COLS), F32)
+            for j in range(lon_count):
+                taken = jnp.take_along_axis(folds[j, 0:8, :], lane, axis=1)
+                picked = jnp.where(block == j, taken, picked)
+            recvs[NORTH][0:8, :] = picked
+            if phase == 0:
                 picked = jnp.zeros((8, COLS), F32)
                 for j in range(lon_count):
-                    taken = jnp.take_along_axis(folds[j, rows, :], lane, axis=1)
+                    counts = jnp.broadcast_to(folds[j, 8:9, :], (8, COLS))
+                    taken = jnp.take_along_axis(counts, lane, axis=1)
                     picked = jnp.where(block == j, taken, picked)
-                recvs[NORTH, rows, :] = picked
+                recvs[NORTH][8:9, :] = picked[0:1]
 
     def finish_phase(phase, sends, recvs, folds):
         to_side(phase, EAST, sends, recvs).wait_send()
@@ -232,20 +265,23 @@
             others = folds.at[pl.ds(0, lon_count - 1)]
             pltpu.make_async_copy(others, others, fold_send.at[phase]).wait()
 
-    def pack(ext, sends, at):
+    def pack_beside(ext, sends, at):
         turned = ext[:, 8:24, :].reshape(COLS, COLS).T
-        sends[EAST, at : at + 8, :] = turned[COLS - 8 :]
-        sends[WEST, at : at + 8, :] = turned[:8]
-        sends[NORTH, at : at + 8, :] = ext[:, 23, :]
-        sends[SOUTH, at : at + 8, :] = ext[:, 8, :]
-
-    def unpack(ext, recvs, at):
-        ext[:, 24, :] = recvs[NORTH, at : at + 8, :]
-        ext[:, 7, :] = recvs[SOUTH, at : at + 8, :]
+        sends[EAST][at : at + 8, :] = turned[COLS - 8 :]
+        sends[WEST][at : at + 8, :] = turned[:8]
+
+    def pack(ext, sends):
+        pack_beside(ext, sends, 0)
+        sends[NORTH][0:8, :] = ext[:, 23, :]
+        sends[SOUTH][0:8, :] = ext[:, 8, :]
+
+    def unpack(ext, recvs):
+        ext[:, 24, :] = recvs[NORTH][0:8, :]
+        ext[:, 7, :] = recvs[SOUTH][0:8, :]
 
     def edge_columns(recvs, at):
-        first = pltpu.roll(recvs[WEST, at : at + 8, :], 1, 0)
-        last = pltpu.roll(recvs[EAST, at : at + 8, :], 7, 0)
+        first = pltpu.roll(recvs[WEST][at : at + 8, :], 1, 0)
+        last = pltpu.roll(recvs[EAST][at : at + 8, :], 7, 0)
         middle = jnp.zeros((COLS - 16, COLS), F32)
         return jnp.concatenate([first, middle, last], axis=0).T.reshape(FIELDS, ROWS, COLS)
 
@@ -279,9 +315,11 @@
                     store_feature(feats, chunk, 4 + t, vertical[k] if k < NZ - 1 else zero)
 
     def halo_features(recvs, feats):
-        north, south = recvs[NORTH, 0:8, :], recvs[SOUTH, 0:8, :]
+        north, south = recvs[NORTH][0:8, :], recvs[SOUTH][0:8, :]
         first = sub8 < NZ
-        wet = jnp.where(first, recv0[NORTH, 16:24, :], pltpu.roll(recv0[SOUTH, 16:24, :], 4, 0))
+        depths = [jnp.broadcast_to(recv0[side][8:9, :], (8, COLS)) for side in (NORTH, SOUTH)]
+        level = lax.rem(sub8, NZ).astype(F32)
+        wet = (level < jnp.where(first, *depths)).astype(F32)
         joint = jnp.where(
             lax.rem(sub8, NZ) == NZ - 1, 0.0, wet * pltpu.roll(wet, 7, 0)
         )
@@ -295,7 +333,7 @@
             store_feature(feats, CHUNKS, 2 + t, -pltpu.roll(vertical, 1, 0))
             store_feature(feats, CHUNKS, 4 + t, vertical)
         column_features(
-            recvs[EAST, 0:1, :], recvs[WEST, 7:8, :], edge_wet(), feats, CHUNKS + 1
+            recvs[EAST][0:1, :], recvs[WEST][7:8, :], edge_wet(), feats, CHUNKS + 1
         )
         return wet
 
@@ -321,10 +359,10 @@
             feats[chunk, 4 + t : 5 + t, :] = vertical[0:1]
 
     def edge_wet():
-        return paired(recv0[EAST, 16:17, :], recv0[WEST, 23:24, :])[0]
+        return paired(recv0[EAST][8:9, :], recv0[WEST][15:16, :])[0]
 
     def own_edge_wet():
-        return paired(send0[EAST, 23:24, :], send0[WEST, 16:17, :])[0]
+        return paired(send0[EAST][15:16, :], send0[WEST][8:9, :])[0]
 
     def wide(x, n):
         return jnp.concatenate([x] * n, axis=1) if n > 1 else x
@@ -363,18 +401,19 @@
         closure_own(feats, h1_ref, h2_ref)
         if phase == 1:
             column_features(
-                sends[EAST, 7:8, :], sends[WEST, 0:1, :], own_edge_wet(), feats, CHUNKS + 2
+                sends[EAST][7:8, :], sends[WEST][0:1, :], own_edge_wet(), feats, CHUNKS + 2
             )
             closure_chunk(feats, CHUNKS + 2, 1, h1_edge, h2_edge, 0)
         wait_phase(phase, sends, recvs, folds)
-        unpack(state, recvs, 0)
+        unpack(state, recvs)
         if phase == 0:
-            unpack(adj0, recvs, 8)
-            unpack(wet_ext, recvs, 16)
+            for k in range(NZ):
+                wet_ext[k, 24:25, :] = (recvs[NORTH][8:9, :] > k).astype(F32)
+                wet_ext[k, 7:8, :] = (recvs[SOUTH][8:9, :] > k).astype(F32)
             wet = wet_ext[:NZ, 8:24, :]
-            around = sides(wet_ext, edge_columns(recvs, 16))
+            around = sides(wet_ext.at[pl.ds(0, NZ)], edge_columns(recvs, 8)[:NZ])
             for n in range(4):
-                pair[n] = 0.5 * wet * around[n][:NZ]
+                pair[n] = 0.5 * wet * around[n]
         wet_halo = halo_features(recvs, feats)
         closure_chunk(feats, CHUNKS, 8, None, None)
         closure_chunk(feats, CHUNKS + 1, 1, None, None)
@@ -405,9 +444,9 @@
             change = change + jnp.concatenate([weight, weight], 0) * difference
         return core + change
 
-    def pull_flux(adjoint, recvs, at, contrast, coef, slope):
+    def pull_flux(adjoint, recvs, contrast, coef, slope):
         core = adjoint[:, 8:24, :]
-        around = sides(adjoint, edge_columns(recvs, at))
+        around = sides(adjoint, edge_columns(recvs, 0))
         total_direct = core
         kappa_bar = jnp.zeros((NZ, ROWS, COLS), F32)
         for n in range(4):
@@ -477,7 +516,7 @@
                     value = value + vertical[k - 1]
                 for t in range(2):
                     i = NZ * t + k
-                    sends[side, i : i + 1, :] = value[t : t + 1] + direct[i, y : y + 1, :]
+                    sends[side][i : i + 1, :] = value[t : t + 1] + direct[i, y : y + 1, :]
         cells = d[2 * NZ]
         vertical = pltpu.roll(cells, 4, 0) - pltpu.roll(pltpu.roll(cells, 6, 0), COLS - ROWS, 1)
         vertical = vertical * joint_column(own_edge_wet())
@@ -487,8 +526,8 @@
         turned = direct[...].reshape(COLS, COLS).T
         from_east = turned[COLS - 1 :] + jnp.where(first, value[0:1], other[1:2])
         from_west = turned[0:1] + jnp.where(first, other[0:1], value[1:2])
-        sends[EAST] = jnp.broadcast_to(from_east, (8, COLS))
-        sends[WEST] = jnp.broadcast_to(from_west, (8, COLS))
+        sends[EAST][...] = jnp.broadcast_to(from_east, (8, COLS))
+        sends[WEST][...] = jnp.broadcast_to(from_west, (8, COLS))
 
     def pull_features():
         @pl.loop(0, CHUNKS, unroll=CHUNKS)
@@ -527,21 +566,27 @@
                         value = value + vertical[k - 1]
                     store(NZ * t + k, half, value)
 
-    depth_here = land[...] * levels[...]
+    loads[0].wait()
+    loads[1].wait()
+    depth_here = land_here[...] * levels_here[...]
     for k in range(NZ):
         wet = (k < depth_here).astype(F32)
         wet_ext[k, 8:24, :] = wet
         wet_ext[NZ + k, 8:24, :] = wet
-    pack(wet_ext, send0, 16)
-    loads[0].wait()
-    pack(state0, send0, 0)
-    loads[1].wait()
-    pack(adj0, send0, 8)
+    pack_beside(wet_ext, send0, 8)
+    depths = depth_here.astype(F32)
+    send0[NORTH][8:9, :] = depths[ROWS - 1 :]
+    send0[SOUTH][8:9, :] = depths[0:1]
+    loads[2].wait()
+    pack(state0, send0)
 
     @pl.when(at_bottom)
     def _():
-        for recvs in (recv0, recv1, recv2):
-            recvs[SOUTH] = jnp.zeros(recvs.shape[1:], F32)
+        for recvs in (recv0, recv1, recv2, recv3):
+            recvs[SOUTH][...] = jnp.zeros(recvs[SOUTH].shape, F32)
+
+    for copy in loads[3:]:
+        copy.wait()
 
     @pl.when(jnp.logical_not(at_top))
     def _():
@@ -552,9 +597,11 @@
         pl.semaphore_wait(barrier, greeted + lon_count - 1)
 
     start_phase(0, send0, recv0, fold0)
-
-    w1_rows[0:6, :] = w_first[...]
-    w1_rows[6:7, :] = b_first[...]
+    pack(adj0, send3)
+    start_phase(3, send3, recv3, fold3)
+
+    w1_rows[0:6, :] = w1_here[...]
+    w1_rows[6:7, :] = b1_here[...]
     w1_rows[7:8, :] = jnp.zeros((1, HID), F32)
     w1 = w1_rows[...]
     w1_high = w1.astype(BF16).astype(F32)
@@ -567,13 +614,13 @@
     w1_high = jnp.concatenate([w1_high, blank], axis=0).astype(BF16)
     w1_low = jnp.concatenate([w1_low, blank], axis=0).astype(BF16)
     w1_bwd[...] = jnp.concatenate([w1_high, w1_high, w1_low], axis=1)
-    w2 = w_second[...]
+    w2 = w2_here[...]
     high, low = halves(w2)
     w2_bwd[...] = jnp.concatenate([high, high, low], axis=1)
     high, low = halves(w2.T)
     w2_fwd[...] = jnp.concatenate([high, high, low], axis=1)
-    bias2[...] = column(b_second[...])
-    head[...] = column(w_head[...])
+    bias2[...] = column(b2_here[...])
+    head[...] = column(wh_here[...])
     ones_row = jnp.where(sub8 == 6, 1.0, 0.0)
     for feats in (feats0, feats1):
         for chunk in range(CHUNKS + 1):
@@ -589,13 +636,15 @@
     state1[:, 8:24, :] = advance(
         0, state0, feats0, send0, recv0, fold0, h1_0, h2_0, kap0, slope0, contrast0, coef0
     )
-    pack(state1, send1, 0)
+    pack(state1, send1)
     start_phase(1, send1, recv1, fold1)
     tracers_out[...] = advance(
         1, state1, feats1, send1, recv1, fold1, h1_1, h2_1, kap1, slope1, contrast1, coef1
     )
 
-    pull_flux(adj0, recv0, 8, contrast1, coef1, slope1)
+    wait_phase(3, send3, recv3, fold3)
+    unpack(adj0, recv3)
+    pull_flux(adj0, recv3, contrast1, coef1, slope1)
     send_edges(h1_1, h2_1, send2)
     start_phase(2, send2, recv2, fold2)
     pull_closure(h1_1, h2_1)
@@ -607,8 +656,8 @@
     pull_state(keep)
     add_weights(feats1, h1_1)
     wait_phase(2, send2, recv2, fold2)
-    unpack(adj1, recv2, 0)
-    pull_flux(adj1, recv2, 0, contrast0, coef0, slope0)
+    unpack(adj1, recv2)
+    pull_flux(adj1, recv2, contrast0, coef0, slope0)
     pull_closure(h1_0, h2_0)
     add_weights(feats0, h1_0)
 
@@ -679,6 +728,7 @@
     finish_phase(0, send0, recv0, fold0)
     finish_phase(1, send1, recv1, fold1)
     finish_phase(2, send2, recv2, fold2)
+    finish_phase(3, send3, recv3, fold3)
     wait_all(parts_plane, plane - 1, sum_send.at[0])
     wait_all(parts_pillar, pillar - 1, sum_send.at[1])
     wait_all(gathered, plane - 1, sum_send.at[2])
@@ -730,35 +780,43 @@
         pltpu.VMEM((16, 2 * HID), F32),
         pltpu.VMEM((HID, COLS), F32),
     ]
-    scratch += [pltpu.VMEM((4, n, COLS), F32) for n in (24, 8, 8)] * 2
-    scratch += [pltpu.VMEM((lon_count, n, COLS), F32) for n in (24, 8, 8)]
+    scratch += [pltpu.VMEM((3, 2, 8, COLS), F32)] * 4
+    scratch += [pltpu.VMEM((2, 16, COLS), F32)] * 2 + [pltpu.VMEM((2, 9, COLS), F32)] * 2
+    scratch += [pltpu.VMEM((lon_count, 9, COLS), F32), pltpu.VMEM((3, lon_count, 8, COLS), F32)]
     scratch += [
         pltpu.VMEM((plane, both, COLS), F32),
         pltpu.VMEM((plane, both, COLS), F32),
         pltpu.VMEM((pillar, both, COLS), F32),
         pltpu.VMEM((plane, both, COLS), F32),
         pltpu.VMEM((8, COLS), F32),
-        pltpu.SemaphoreType.DMA((3, 4)),
-        pltpu.SemaphoreType.DMA((3, 4)),
+        pltpu.SemaphoreType.DMA((4, 4)),
+        pltpu.SemaphoreType.DMA((4, 4)),
+        pltpu.SemaphoreType.DMA((4,)),
+        pltpu.SemaphoreType.DMA((4,)),
         pltpu.SemaphoreType.DMA((3,)),
         pltpu.SemaphoreType.DMA((3,)),
-        pltpu.SemaphoreType.DMA((3,)),
-        pltpu.SemaphoreType.DMA((3,)),
-        pltpu.SemaphoreType.DMA((2,)),
+        pltpu.SemaphoreType.DMA((10,)),
+        pltpu.VMEM((ROWS, COLS), jnp.int32),
+        pltpu.VMEM((ROWS, COLS), jnp.int32),
+        pltpu.VMEM((1, COLS), jnp.int32),
+        pltpu.VMEM((6, HID), F32),
+        pltpu.VMEM((1, HID), F32),
+        pltpu.VMEM((HID, HID), F32),
+        pltpu.VMEM((1, HID), F32),
+        pltpu.VMEM((1, HID), F32),
     ]
     vmem = pl.BlockSpec(memory_space=pltpu.VMEM)
     anywhere = pl.BlockSpec(memory_space=pl.ANY)
     run = pl.pallas_call(
         lambda *refs: kernel(lat_count, lon_count, *refs),
         out_shape=[
-            jax.ShapeDtypeStruct(field, F32),
-            jax.ShapeDtypeStruct(field, F32),
-            jax.ShapeDtypeStruct((6, HID), F32),
-            jax.ShapeDtypeStruct((HID, HID), F32),
-            jax.ShapeDtypeStruct((1, HID), F32),
+            pltpu.VMEM(field, F32),
+            pltpu.VMEM(field, F32),
+            pltpu.VMEM((6, HID), F32),
+            pltpu.VMEM((HID, HID), F32),
+            pltpu.VMEM((1, HID), F32),
         ],
-        in_specs=[anywhere] + [vmem] * 3 + [anywhere] + [vmem] * 5
-        + [pl.BlockSpec(memory_space=pltpu.SMEM)],
+        in_specs=[anywhere] * 10 + [pl.BlockSpec(memory_space=pltpu.SMEM)],
         out_specs=[vmem] * 5,
         scratch_shapes=scratch,
         compiler_params=pltpu.CompilerParams(
@@ -777,7 +835,7 @@
         in_specs=[vmem] * 5,
         out_specs=[vmem] * 5,
         name="hand_over",
-    )(*results)
+    )(*(pltpu.with_memory_space_constraint(r, pltpu.VMEM) for r in results))
     return (
         out.reshape(tracers.shape), grad.reshape(tracers.shape), first, second, head.reshape(HID)
     )

time: 50.7 us -> 48.6 us (0.959)
  Pallas kernels: 49.1 us -> 47.2 us
    pallas_call x1, Pallas kernels: 47.6 us -> 46.5 us  [per_device(): run(tracers.reshape(field), land_mask, level_counts, fold_partner.reshape...]
    pallas_call x1, Pallas kernels: 1.59 us -> 0.69 us  [per_device(): pl.pallas_call(hand_over, out_shape=[jax.ShapeDtypeStruct(r.shape, F32) f...]
where the time goes in v4:
time: 48.6 us; the launch traced here: 48.5 us
  Pallas kernels  47.2 us (97%)
  between operations  1.29 us (3%)
    pallas_call x1, Pallas kernels, per_device(): run(tracers.reshape(field), land_mask, level_counts, fold_partner.reshape...  46.5 us

profile of v4, /device:TPU:1, one launch (start us, length us, event | category | flops | bytes accessed | tf_op | source)
XLA Modules:
  0.0 48.5 jit_solution(3456952506277802946)
XLA Ops:
  1.3 46.5 %adjoint_steps.1 = (f32[8,16,128]{2,1,0:T(8,128)S(1)}, f32[8,16,128]{2,1,0:T(8,128)S(1)}, f32[6,128]{1,0:T(8,128)S(1)}, f32[128,128]{1,0:T(8,128)S(1)}, f32[1,128]{1,0:T(1,128)S(1)}) custom-call(f32[8,16,128]{2,1,0:T(8,128)} %bitcast.9, s32[16,128]{1,0:T(8,128)} %refs_1_.1, s32[16,128]{1,0:T(8,128)} %refs_2_.1, s32[1,128]{1,0:T(1,128)} %bitcast.11, ...), custom_call_target="tpu_custom_call" | custom-call | tf_op jit(solution)/shard_map/adjoint_steps/pallas_call | solution.py:827
  47.8 0.7 %hand_over.1 = (f32[8,16,128]{2,1,0:T(8,128)}, f32[8,16,128]{2,1,0:T(8,128)}, f32[6,128]{1,0:T(8,128)}, f32[128,128]{1,0:T(8,128)}, f32[1,128]{1,0:T(1,128)}) custom-call(f32[8,16,128]{2,1,0:T(8,128)S(1)} %get-tuple-element.15.refs_0_, f32[8,16,128]{2,1,0:T(8,128)S(1)} %get-tuple-element.16.refs_1_, f32[6,128]{1,0:T(8,128)S(1)} %get-tuple-element.17.refs_2_, ...), custom_call_target="tpu_custom_call" | custom-call | tf_op jit(solution)/shard_map/hand_over/pallas_call | solution.py:832

commit v5 on v4

--- a/solution.py
+++ b/solution.py
@@ -80,8 +80,8 @@
     tracers_out, tracer_grad, gw_first, gw_second, gw_head,
     w1_rows, w1_fwd, w1_bwd, w2_fwd, w2_bwd, bias2, head,
     wet_ext, pair, state0, state1, adj0, adj1, kap0, kap1, contrast0, contrast1, coef0, coef1,
-    slope0, slope1, direct, feats0, feats1, logits, h1_0, h1_1, h2_0, h2_1, dz2, dz1,
-    h1_edge, h2_edge, dfeat,
+    slope0, slope1, direct, feats0, feats1, logits, h1_0, h1_1, h2_0, h2_1,
+    u2_0, u2_1, u1_0, u1_1, by_feat0, by_feat1,
     obar, acc2, acc1, acch,
     beside_out, beside_in, across_out, across_in, wet_beside_out, wet_beside_in, first_out, first_in,
     fold_first, folded,
@@ -361,15 +361,10 @@
     def edge_wet():
         return paired(recv0[EAST][8:9, :], recv0[WEST][15:16, :])[0]
 
-    def own_edge_wet():
-        return paired(send0[EAST][15:16, :], send0[WEST][8:9, :])[0]
-
     def wide(x, n):
         return jnp.concatenate([x] * n, axis=1) if n > 1 else x
 
-    def closure_chunk(feats, chunk, rows, h1_ref, h2_ref, at=None):
-        at = chunk if at is None else at
-        n = rows
+    def closure_chunk(feats, chunk, n, keep=None):
         f = [feats[chunk, 8 * q : 8 * q + 8, :] for q in range(n)]
         f = jnp.concatenate(f, axis=1) if n > 1 else f[0]
         high = f.astype(BF16).astype(F32)
@@ -382,28 +377,35 @@
         o = jnp.sum(h2 * wide(head[...], n), axis=0, keepdims=True)
         for q in range(n):
             logits[chunk, q : q + 1, :] = o[:, COLS * q : COLS * (q + 1)]
-        if h1_ref is not None:
-            h1_ref[at, :HID, :] = h1_high
-            h1_ref[at, HID:, :] = h1_low
-            h2_ref[at] = h2
-
-    def closure_own(feats, h1_ref, h2_ref):
+        if keep is None:
+            return
+        h1_ref, h2_ref, u2_ref, u1_ref, by_feat = keep
+        h1_ref[chunk, :HID, :] = h1_high
+        h1_ref[chunk, HID:, :] = h1_low
+        h2_ref[chunk] = h2
+        u2 = wide(head[...], n) * (1.0 - h2 * h2)
+        u2_ref[chunk] = u2
+        u2_high, u2_low = halves(u2)
+        by_h1 = dot(w2_bwd[...], jnp.concatenate([u2_high, u2_low, u2_high], axis=0))
+        u1_high, u1_low = halves(by_h1 * (1.0 - h1 * h1))
+        u1_ref[chunk, :HID, :] = u1_high
+        u1_ref[chunk, HID:, :] = u1_low
+        d = dot(w1_bwd[...], jnp.concatenate([u1_high, u1_low, u1_high], axis=0))
+        for q in range(n):
+            by_feat[chunk, 8 * q : 8 * q + 8, :] = d[:8, COLS * q : COLS * (q + 1)]
+
+    def closure_own(feats, keep):
         @pl.loop(0, CHUNKS, unroll=CHUNKS)
         def _(chunk):
-            closure_chunk(feats, chunk, 8, h1_ref, h2_ref)
+            closure_chunk(feats, chunk, 8, keep)
 
     def kappa_from(o, wet):
         gate = jax.nn.sigmoid(o + b_head[0])
         return KMAX * gate * wet, KMAX * gate * (1.0 - gate) * wet
 
-    def advance(phase, state, feats, sends, recvs, folds, h1_ref, h2_ref, kap, slope, contrast, coef):
+    def advance(phase, state, feats, sends, recvs, folds, keep, kap, slope, contrast, coef):
         own_features(state, feats)
-        closure_own(feats, h1_ref, h2_ref)
-        if phase == 1:
-            column_features(
-                sends[EAST][7:8, :], sends[WEST][0:1, :], own_edge_wet(), feats, CHUNKS + 2
-            )
-            closure_chunk(feats, CHUNKS + 2, 1, h1_edge, h2_edge, 0)
+        closure_own(feats, keep)
         wait_phase(phase, sends, recvs, folds)
         unpack(state, recvs)
         if phase == 0:
@@ -415,8 +417,8 @@
             for n in range(4):
                 pair[n] = 0.5 * wet * around[n]
         wet_halo = halo_features(recvs, feats)
-        closure_chunk(feats, CHUNKS, 8, None, None)
-        closure_chunk(feats, CHUNKS + 1, 1, None, None)
+        closure_chunk(feats, CHUNKS, 8)
+        closure_chunk(feats, CHUNKS + 1, 1)
         for k in range(NZ):
             for half in range(2):
                 rows = pl.ds(8 + 8 * half, 8)
@@ -458,101 +460,33 @@
         direct[...] = total_direct
         obar[...] = kappa_bar.reshape(CHUNKS, 8, COLS) * slope[...]
 
-    def pull_cells(bar, h1_high, h1_low, h2):
-        n = bar.shape[1] // COLS
-        weighted = h2 * bar
-        d2_high, d2_low = halves(wide(head[...], n) * (bar - weighted * h2))
-        dh1 = dot(w2_bwd[...], jnp.concatenate([d2_high, d2_low, d2_high], axis=0))
-        h1 = h1_high.astype(F32) + h1_low.astype(F32)
-        d1_high, d1_low = halves(dh1 * (1.0 - h1 * h1))
-        return weighted, d2_high, d2_low, d1_high, d1_low
-
-    def pull_closure(h1_ref, h2_ref):
+    def add_weights(feats, keep):
+        h1_ref, h2_ref, u2_ref, u1_ref, _ = keep
+
         @pl.loop(0, CHUNKS, unroll=CHUNKS)
         def _(chunk):
             bar = jnp.concatenate([obar[chunk, q : q + 1, :] for q in range(8)], axis=1)
-            weighted, d2_high, d2_low, d1_high, d1_low = pull_cells(
-                bar, h1_ref[chunk, :HID, :], h1_ref[chunk, HID:, :], h2_ref[chunk]
-            )
-            dz2[chunk, :HID, :] = d2_high
-            dz2[chunk, HID:, :] = d2_low
-            dz1[chunk, :HID, :] = d1_high
-            dz1[chunk, HID:, :] = d1_low
+            high, low = halves(u2_ref[chunk] * bar)
+            acc2[...] += dot_nt(h1_ref[chunk], jnp.concatenate([high, low], axis=0))
+            f = jnp.concatenate([feats[chunk, 8 * q : 8 * q + 8, :] for q in range(8)], axis=1)
+            f = f * bar
+            high = f.astype(BF16).astype(F32)
+            stacked = jnp.concatenate([high, f - high], axis=0).astype(BF16)
+            acc1[...] += dot_nt(stacked, u1_ref[chunk])
+            weighted = h2_ref[chunk] * bar
             heads = weighted[:, :COLS]
             for q in range(1, 8):
                 heads = heads + weighted[:, COLS * q : COLS * (q + 1)]
             acch[...] += heads
 
-    def send_edges(h1_ref, h2_ref, sends):
-        tops = [(2 * k + 1, 7) for k in range(NZ)]
-        lows = [(2 * k, 0) for k in range(NZ)]
-        places = tops + lows
-        turned = jnp.concatenate(
-            [obar[...].reshape(HALF, COLS), jnp.zeros((HALF, COLS), F32)], axis=0
-        ).T
-        column_bar = paired(turned[COLS - 1 :], turned[0:1])[0][0:1]
-        bar = jnp.concatenate([obar[c, q : q + 1, :] for c, q in places] + [column_bar], axis=1)
-        cut = [slice(COLS * q, COLS * (q + 1)) for _, q in places]
-        high = [h1_ref[c, :HID, l] for (c, _), l in zip(places, cut)] + [h1_edge[0, :HID, :]]
-        low = [h1_ref[c, HID:, l] for (c, _), l in zip(places, cut)] + [h1_edge[0, HID:, :]]
-        h2 = [h2_ref[c, :, l] for (c, _), l in zip(places, cut)] + [h2_edge[0]]
-        high, low, h2 = (jnp.concatenate(x, axis=1) for x in (high, low, h2))
-        _, _, _, d1_high, d1_low = pull_cells(bar, high, low, h2)
-        d = dot(w1_bwd[...], jnp.concatenate([d1_high, d1_low, d1_high], axis=0))
-        d = [d[:8, COLS * i : COLS * (i + 1)] for i in range(len(places) + 1)]
-        for side, y in ((NORTH, ROWS - 1), (SOUTH, 0)):
-            rows = d[:NZ] if side == NORTH else d[NZ : 2 * NZ]
-            wets = [wet_ext[k, 8 + y : 9 + y, :] for k in range(NZ)]
-            vertical = [
-                (pltpu.roll(rows[k], 4, 0) - pltpu.roll(rows[k + 1], 6, 0))
-                * (wets[k + 1] * wets[k])
-                for k in range(NZ - 1)
-            ]
-            for k in range(NZ):
-                value = rows[k]
-                if k < NZ - 1:
-                    value = value - vertical[k]
-                if k > 0:
-                    value = value + vertical[k - 1]
-                for t in range(2):
-                    i = NZ * t + k
-                    sends[side][i : i + 1, :] = value[t : t + 1] + direct[i, y : y + 1, :]
-        cells = d[2 * NZ]
-        vertical = pltpu.roll(cells, 4, 0) - pltpu.roll(pltpu.roll(cells, 6, 0), COLS - ROWS, 1)
-        vertical = vertical * joint_column(own_edge_wet())
-        value = cells - vertical + pltpu.roll(vertical, ROWS, 1)
-        other = pltpu.roll(value, HALF, 1)
-        first = lane8[0:1] < HALF
-        turned = direct[...].reshape(COLS, COLS).T
-        from_east = turned[COLS - 1 :] + jnp.where(first, value[0:1], other[1:2])
-        from_west = turned[0:1] + jnp.where(first, other[0:1], value[1:2])
-        sends[EAST][...] = jnp.broadcast_to(from_east, (8, COLS))
-        sends[WEST][...] = jnp.broadcast_to(from_west, (8, COLS))
-
-    def pull_features():
-        @pl.loop(0, CHUNKS, unroll=CHUNKS)
-        def _(chunk):
-            d1 = dz1[chunk]
-            d = dot(w1_bwd[...], jnp.concatenate([d1, d1[:HID]], axis=0))
-            for q in range(8):
-                dfeat[chunk, 8 * q : 8 * q + 8, :] = d[:8, COLS * q : COLS * (q + 1)]
-
-    def add_weights(feats, h1_ref):
-        @pl.loop(0, CHUNKS, unroll=CHUNKS)
-        def _(chunk):
-            acc2[...] += dot_nt(h1_ref[chunk], dz2[chunk])
-            f = jnp.concatenate([feats[chunk, 8 * q : 8 * q + 8, :] for q in range(8)], axis=1)
-            high = f.astype(BF16).astype(F32)
-            stacked = jnp.concatenate([high, f - high], axis=0).astype(BF16)
-            acc1[...] += dot_nt(stacked, dz1[chunk])
-
-    def pull_state(store):
+    def pull_state(by_feat, store):
         for half in range(2):
             rows = pl.ds(8 * half, 8)
             wets = [wet_ext[k, pl.ds(8 + 8 * half, 8), :] for k in range(NZ)]
+            bars = [obar[2 * k + half] for k in range(NZ)]
             for t in range(2):
                 bar = [
-                    [dfeat[2 * k + half, pl.ds(f, 8, stride=8), :] for k in range(NZ)]
+                    [by_feat[2 * k + half, pl.ds(f, 8, stride=8), :] * bars[k] for k in range(NZ)]
                     for f in (t, 2 + t, 4 + t)
                 ]
                 vertical = [
@@ -627,39 +561,38 @@
             feats[chunk, pl.ds(6, 8, stride=8), :] = jnp.ones((8, COLS), F32)
             feats[chunk, pl.ds(7, 8, stride=8), :] = jnp.zeros((8, COLS), F32)
         feats[CHUNKS + 1, 0:8, :] = ones_row
-        feats[CHUNKS + 2, 0:8, :] = ones_row
     logits[CHUNKS + 1] = jnp.zeros((8, COLS), F32)
     acc2[...] = jnp.zeros_like(acc2)
     acc1[...] = jnp.zeros_like(acc1)
     acch[...] = jnp.zeros_like(acch)
 
+    keep0 = (h1_0, h2_0, u2_0, u1_0, by_feat0)
+    keep1 = (h1_1, h2_1, u2_1, u1_1, by_feat1)
+
     state1[:, 8:24, :] = advance(
-        0, state0, feats0, send0, recv0, fold0, h1_0, h2_0, kap0, slope0, contrast0, coef0
+        0, state0, feats0, send0, recv0, fold0, keep0, kap0, slope0, contrast0, coef0
     )
     pack(state1, send1)
     start_phase(1, send1, recv1, fold1)
     tracers_out[...] = advance(
-        1, state1, feats1, send1, recv1, fold1, h1_1, h2_1, kap1, slope1, contrast1, coef1
+        1, state1, feats1, send1, recv1, fold1, keep1, kap1, slope1, contrast1, coef1
     )
 
     wait_phase(3, send3, recv3, fold3)
     unpack(adj0, recv3)
     pull_flux(adj0, recv3, contrast1, coef1, slope1)
-    send_edges(h1_1, h2_1, send2)
+
+    def store_adjoint(i, half, value):
+        adj1[i, 8 + 8 * half : 16 + 8 * half, :] = value
+
+    pull_state(by_feat1, store_adjoint)
+    pack(adj1, send2)
     start_phase(2, send2, recv2, fold2)
-    pull_closure(h1_1, h2_1)
-    pull_features()
-
-    def keep(i, half, value):
-        adj1[i, 8 + 8 * half : 16 + 8 * half, :] = value
-
-    pull_state(keep)
-    add_weights(feats1, h1_1)
+    add_weights(feats1, keep1)
     wait_phase(2, send2, recv2, fold2)
     unpack(adj1, recv2)
     pull_flux(adj1, recv2, contrast0, coef0, slope0)
-    pull_closure(h1_0, h2_0)
-    add_weights(feats0, h1_0)
+    add_weights(feats0, keep0)
 
     plane = x_count * sizes["y_high"] * y_low_count
     pillar = core_count * sizes["z"]
@@ -695,12 +628,10 @@
     me = share(PLANE, 0, lambda there: parts.at[there], parts_plane)
     parts_plane[me] = parts[me]
 
-    pull_features()
-
     def finish(i, half, value):
         tracer_grad[i, 8 * half : 8 * half + 8, :] = value
 
-    pull_state(finish)
+    pull_state(by_feat0, finish)
 
     wait_all(parts_plane, plane - 1, sum_recv.at[0])
     summed = parts_plane[0]
@@ -744,7 +675,7 @@
     field = (FIELDS, ROWS, COLS)
     ext = pltpu.VMEM((FIELDS, 32, COLS), F32)
     kap = pltpu.VMEM((NZ, 32, COLS), F32)
-    feats = pltpu.VMEM((CHUNKS + 3, 64, COLS), F32)
+    feats = pltpu.VMEM((CHUNKS + 2, 64, COLS), F32)
     stack = pltpu.VMEM((CHUNKS, 2 * HID, LANES), BF16)
     dense = pltpu.VMEM((CHUNKS, HID, LANES), F32)
     tile = pltpu.VMEM((CHUNKS, 8, COLS), F32)
@@ -770,10 +701,9 @@
         tile, tile,
         pltpu.VMEM(field, F32),
         feats, feats,
-        pltpu.VMEM((CHUNKS + 3, 8, COLS), F32),
-        stack, stack, dense, dense, stack, stack,
-        pltpu.VMEM((1, 2 * HID, COLS), BF16),
-        pltpu.VMEM((1, HID, COLS), F32),
+        pltpu.VMEM((CHUNKS + 2, 8, COLS), F32),
+        stack, stack, dense, dense, dense, dense, stack, stack,
+        pltpu.VMEM((CHUNKS, 64, COLS), F32),
         pltpu.VMEM((CHUNKS, 64, COLS), F32),
         tile,
         pltpu.VMEM((2 * HID, 2 * HID), F32),

time: 48.6 us -> 49.1 us (1.010)
  no operation moved by 1% of the time
where the time goes in v5:
time: 49.1 us; the launch traced here: 48.9 us
  Pallas kernels  47.6 us (97%)
  between operations  1.29 us (3%)
    pallas_call x1, Pallas kernels, per_device(): run(tracers.reshape(field), land_mask, level_counts, fold_partner.reshape...  46.9 us

profile of v5, /device:TPU:1, one launch (start us, length us, event | category | flops | bytes accessed | tf_op | source)
XLA Modules:
  0.0 48.9 jit_solution(17311518420639088748)
XLA Ops:
  1.3 46.9 %adjoint_steps.1 = (f32[8,16,128]{2,1,0:T(8,128)S(1)}, f32[8,16,128]{2,1,0:T(8,128)S(1)}, f32[6,128]{1,0:T(8,128)S(1)}, f32[128,128]{1,0:T(8,128)S(1)}, f32[1,128]{1,0:T(1,128)S(1)}) custom-call(f32[8,16,128]{2,1,0:T(8,128)} %bitcast.9, s32[16,128]{1,0:T(8,128)} %refs_1_.1, s32[16,128]{1,0:T(8,128)} %refs_2_.1, s32[1,128]{1,0:T(1,128)} %bitcast.11, ...), custom_call_target="tpu_custom_call" | custom-call | tf_op jit(solution)/shard_map/adjoint_steps/pallas_call | solution.py:757
  48.2 0.7 %hand_over.1 = (f32[8,16,128]{2,1,0:T(8,128)}, f32[8,16,128]{2,1,0:T(8,128)}, f32[6,128]{1,0:T(8,128)}, f32[128,128]{1,0:T(8,128)}, f32[1,128]{1,0:T(1,128)}) custom-call(f32[8,16,128]{2,1,0:T(8,128)S(1)} %get-tuple-element.15.refs_0_, f32[8,16,128]{2,1,0:T(8,128)S(1)} %get-tuple-element.16.refs_1_, f32[6,128]{1,0:T(8,128)S(1)} %get-tuple-element.17.refs_2_, ...), custom_call_target="tpu_custom_call" | custom-call | tf_op jit(solution)/shard_map/hand_over/pallas_call | solution.py:762

commit v6 on v5

--- a/solution.py
+++ b/solution.py
@@ -59,6 +59,12 @@
 
 def dot(a, b):
     return jnp.dot(a, b, preferred_element_type=F32)
+
+
+def product(weights, high, low):
+    both = dot(weights[...], jnp.concatenate([high, low], axis=0))
+    half = both.shape[0] // 2
+    return both[:half] + both[half:]
 
 
 def dot_nt(a, b):
@@ -372,7 +378,7 @@
         stacked = jnp.concatenate([high, low, high, low], axis=0).astype(BF16)
         h1 = jnp.tanh(dot(w1_fwd[...], stacked))
         h1_high, h1_low = halves(h1)
-        pre2 = dot(w2_fwd[...], jnp.concatenate([h1_high, h1_low, h1_high], axis=0))
+        pre2 = product(w2_fwd, h1_high, h1_low)
         h2 = jnp.tanh(pre2 + wide(bias2[...], n))
         o = jnp.sum(h2 * wide(head[...], n), axis=0, keepdims=True)
         for q in range(n):
@@ -386,13 +392,13 @@
         u2 = wide(head[...], n) * (1.0 - h2 * h2)
         u2_ref[chunk] = u2
         u2_high, u2_low = halves(u2)
-        by_h1 = dot(w2_bwd[...], jnp.concatenate([u2_high, u2_low, u2_high], axis=0))
+        by_h1 = product(w2_bwd, u2_high, u2_low)
         u1_high, u1_low = halves(by_h1 * (1.0 - h1 * h1))
         u1_ref[chunk, :HID, :] = u1_high
         u1_ref[chunk, HID:, :] = u1_low
-        d = dot(w1_bwd[...], jnp.concatenate([u1_high, u1_low, u1_high], axis=0))
+        d = product(w1_bwd, u1_high, u1_low)
         for q in range(n):
-            by_feat[chunk, 8 * q : 8 * q + 8, :] = d[:8, COLS * q : COLS * (q + 1)]
+            by_feat[chunk, 8 * q : 8 * q + 8, :] = d[:, COLS * q : COLS * (q + 1)]
 
     def closure_own(feats, keep):
         @pl.loop(0, CHUNKS, unroll=CHUNKS)
@@ -545,14 +551,17 @@
     )
     w1_fwd[...] = tall.T[:, :32].astype(BF16)
     blank = jnp.zeros((8, HID), F32)
-    w1_high = jnp.concatenate([w1_high, blank], axis=0).astype(BF16)
-    w1_low = jnp.concatenate([w1_low, blank], axis=0).astype(BF16)
-    w1_bwd[...] = jnp.concatenate([w1_high, w1_high, w1_low], axis=1)
+    w1_bwd[...] = jnp.concatenate(
+        [jnp.concatenate([w1_high, w1_low], axis=0), jnp.concatenate([w1_high, blank], axis=0)],
+        axis=1,
+    ).astype(BF16)
     w2 = w2_here[...]
-    high, low = halves(w2)
-    w2_bwd[...] = jnp.concatenate([high, high, low], axis=1)
-    high, low = halves(w2.T)
-    w2_fwd[...] = jnp.concatenate([high, high, low], axis=1)
+    for target, matrix in ((w2_bwd, w2), (w2_fwd, w2.T)):
+        high, low = halves(matrix)
+        target[:HID, :HID] = high
+        target[:HID, HID:] = high
+        target[HID:, :HID] = low
+        target[HID:, HID:] = jnp.zeros((HID, HID), BF16)
     bias2[...] = column(b2_here[...])
     head[...] = column(wh_here[...])
     ones_row = jnp.where(sub8 == 6, 1.0, 0.0)
@@ -686,9 +695,9 @@
     scratch = [
         pltpu.VMEM((8, HID), F32),
         pltpu.VMEM((HID, 32), BF16),
-        pltpu.VMEM((16, 3 * HID), BF16),
-        pltpu.VMEM((HID, 3 * HID), BF16),
-        pltpu.VMEM((HID, 3 * HID), BF16),
+        pltpu.VMEM((16, 2 * HID), BF16),
+        pltpu.VMEM((2 * HID, 2 * HID), BF16),
+        pltpu.VMEM((2 * HID, 2 * HID), BF16),
         pltpu.VMEM((HID, COLS), F32),
         pltpu.VMEM((HID, COLS), F32),
         ext,

time: 49.1 us -> 48 us (0.978)
  Pallas kernels: 47.6 us -> 46.5 us
    pallas_call x1, Pallas kernels: 46.9 us -> 45.8 us  [per_device(): run(tracers.reshape(field), land_mask, level_counts, fold_partner.reshape...]
where the time goes in v6:
time: 48 us; the launch traced here: 47.8 us
  Pallas kernels  46.5 us (97%)
  between operations  1.29 us (3%)
    pallas_call x1, Pallas kernels, per_device(): run(tracers.reshape(field), land_mask, level_counts, fold_partner.reshape...  45.8 us

profile of v6, /device:TPU:1, one launch (start us, length us, event | category | flops | bytes accessed | tf_op | source)
XLA Modules:
  0.0 47.8 jit_solution(7662840297269387274)
XLA Ops:
  1.3 45.8 %adjoint_steps.1 = (f32[8,16,128]{2,1,0:T(8,128)S(1)}, f32[8,16,128]{2,1,0:T(8,128)S(1)}, f32[6,128]{1,0:T(8,128)S(1)}, f32[128,128]{1,0:T(8,128)S(1)}, f32[1,128]{1,0:T(1,128)S(1)}) custom-call(f32[8,16,128]{2,1,0:T(8,128)} %bitcast.9, s32[16,128]{1,0:T(8,128)} %refs_1_.1, s32[16,128]{1,0:T(8,128)} %refs_2_.1, s32[1,128]{1,0:T(1,128)} %bitcast.11, ...), custom_call_target="tpu_custom_call" | custom-call | tf_op jit(solution)/shard_map/adjoint_steps/pallas_call | solution.py:766
  47.1 0.7 %hand_over.1 = (f32[8,16,128]{2,1,0:T(8,128)}, f32[8,16,128]{2,1,0:T(8,128)}, f32[6,128]{1,0:T(8,128)}, f32[128,128]{1,0:T(8,128)}, f32[1,128]{1,0:T(1,128)}) custom-call(f32[8,16,128]{2,1,0:T(8,128)S(1)} %get-tuple-element.15.refs_0_, f32[8,16,128]{2,1,0:T(8,128)S(1)} %get-tuple-element.16.refs_1_, f32[6,128]{1,0:T(8,128)S(1)} %get-tuple-element.17.refs_2_, ...), custom_call_target="tpu_custom_call" | custom-call | tf_op jit(solution)/shard_map/hand_over/pallas_call | solution.py:771

commit v7 on v6

--- a/solution.py
+++ b/solution.py
@@ -642,6 +642,12 @@
 
     pull_state(by_feat0, finish)
 
+    finish_phase(0, send0, recv0, fold0)
+    finish_phase(1, send1, recv1, fold1)
+    finish_phase(2, send2, recv2, fold2)
+    finish_phase(3, send3, recv3, fold3)
+    wait_all(parts_plane, plane - 1, sum_send.at[0])
+
     wait_all(parts_plane, plane - 1, sum_recv.at[0])
     summed = parts_plane[0]
     for p in range(1, plane):
@@ -649,6 +655,7 @@
     me = slot(PILLAR, here)
     parts_pillar[me] = summed
     share(PILLAR, 1, lambda there: parts_pillar.at[me], parts_pillar)
+    wait_all(parts_pillar, pillar - 1, sum_send.at[1])
     wait_all(parts_pillar, pillar - 1, sum_recv.at[1])
     summed = parts_pillar[0]
     for p in range(1, pillar):
@@ -664,13 +671,6 @@
             extras[spare * p : spare * (p + 1), :] = gathered[p, piece:, :]
     gw_first[...] = extras[0:6, :]
     gw_head[...] = extras[6:7, :]
-
-    finish_phase(0, send0, recv0, fold0)
-    finish_phase(1, send1, recv1, fold1)
-    finish_phase(2, send2, recv2, fold2)
-    finish_phase(3, send3, recv3, fold3)
-    wait_all(parts_plane, plane - 1, sum_send.at[0])
-    wait_all(parts_pillar, pillar - 1, sum_send.at[1])
     wait_all(gathered, plane - 1, sum_send.at[2])
 
 

time: 48 us -> 47.9 us (level)
  no operation moved by 1% of the time
where the time goes in v7:
time: 47.9 us; the launch traced here: 47.8 us
  Pallas kernels  46.5 us (97%)
  between operations  1.29 us (3%)
    pallas_call x1, Pallas kernels, per_device(): run(tracers.reshape(field), land_mask, level_counts, fold_partner.reshape...  45.8 us

profile of v7, /device:TPU:1, one launch (start us, length us, event | category | flops | bytes accessed | tf_op | source)
XLA Modules:
  0.0 47.8 jit_solution(4092189324644219437)
XLA Ops:
  1.3 45.8 %adjoint_steps.1 = (f32[8,16,128]{2,1,0:T(8,128)S(1)}, f32[8,16,128]{2,1,0:T(8,128)S(1)}, f32[6,128]{1,0:T(8,128)S(1)}, f32[128,128]{1,0:T(8,128)S(1)}, f32[1,128]{1,0:T(1,128)S(1)}) custom-call(f32[8,16,128]{2,1,0:T(8,128)} %bitcast.9, s32[16,128]{1,0:T(8,128)} %refs_1_.1, s32[16,128]{1,0:T(8,128)} %refs_2_.1, s32[1,128]{1,0:T(1,128)} %bitcast.11, ...), custom_call_target="tpu_custom_call" | custom-call | tf_op jit(solution)/shard_map/adjoint_steps/pallas_call | solution.py:766
  47.1 0.7 %hand_over.1 = (f32[8,16,128]{2,1,0:T(8,128)}, f32[8,16,128]{2,1,0:T(8,128)}, f32[6,128]{1,0:T(8,128)}, f32[128,128]{1,0:T(8,128)}, f32[1,128]{1,0:T(1,128)}) custom-call(f32[8,16,128]{2,1,0:T(8,128)S(1)} %get-tuple-element.15.refs_0_, f32[8,16,128]{2,1,0:T(8,128)S(1)} %get-tuple-element.16.refs_1_, f32[6,128]{1,0:T(8,128)S(1)} %get-tuple-element.17.refs_2_, ...), custom_call_target="tpu_custom_call" | custom-call | tf_op jit(solution)/shard_map/hand_over/pallas_call | solution.py:771

commit v8 on v7

--- a/solution.py
+++ b/solution.py
@@ -371,7 +371,7 @@
         return jnp.concatenate([x] * n, axis=1) if n > 1 else x
 
     def closure_chunk(feats, chunk, n, keep=None):
-        f = [feats[chunk, 8 * q : 8 * q + 8, :] for q in range(n)]
+        f = [feats[chunk + q // 8, 8 * (q % 8) : 8 * (q % 8) + 8, :] for q in range(n)]
         f = jnp.concatenate(f, axis=1) if n > 1 else f[0]
         high = f.astype(BF16).astype(F32)
         low = f - high
@@ -382,28 +382,32 @@
         h2 = jnp.tanh(pre2 + wide(bias2[...], n))
         o = jnp.sum(h2 * wide(head[...], n), axis=0, keepdims=True)
         for q in range(n):
-            logits[chunk, q : q + 1, :] = o[:, COLS * q : COLS * (q + 1)]
+            logits[chunk + q // 8, q % 8 : q % 8 + 1, :] = o[:, COLS * q : COLS * (q + 1)]
         if keep is None:
             return
         h1_ref, h2_ref, u2_ref, u1_ref, by_feat = keep
-        h1_ref[chunk, :HID, :] = h1_high
-        h1_ref[chunk, HID:, :] = h1_low
-        h2_ref[chunk] = h2
+        parts_of = [slice(LANES * i, LANES * (i + 1)) for i in range(n // 8)]
+        for i, lanes in enumerate(parts_of):
+            h1_ref[chunk + i, :HID, :] = h1_high[:, lanes]
+            h1_ref[chunk + i, HID:, :] = h1_low[:, lanes]
+            h2_ref[chunk + i] = h2[:, lanes]
         u2 = wide(head[...], n) * (1.0 - h2 * h2)
-        u2_ref[chunk] = u2
+        for i, lanes in enumerate(parts_of):
+            u2_ref[chunk + i] = u2[:, lanes]
         u2_high, u2_low = halves(u2)
         by_h1 = product(w2_bwd, u2_high, u2_low)
         u1_high, u1_low = halves(by_h1 * (1.0 - h1 * h1))
-        u1_ref[chunk, :HID, :] = u1_high
-        u1_ref[chunk, HID:, :] = u1_low
+        for i, lanes in enumerate(parts_of):
+            u1_ref[chunk + i, :HID, :] = u1_high[:, lanes]
+            u1_ref[chunk + i, HID:, :] = u1_low[:, lanes]
         d = product(w1_bwd, u1_high, u1_low)
         for q in range(n):
-            by_feat[chunk, 8 * q : 8 * q + 8, :] = d[:, COLS * q : COLS * (q + 1)]
+            rows = slice(8 * (q % 8), 8 * (q % 8) + 8)
+            by_feat[chunk + q // 8, rows, :] = d[:, COLS * q : COLS * (q + 1)]
 
     def closure_own(feats, keep):
-        @pl.loop(0, CHUNKS, unroll=CHUNKS)
-        def _(chunk):
-            closure_chunk(feats, chunk, 8, keep)
+        for chunk in range(0, CHUNKS, 2):
+            closure_chunk(feats, chunk, 16, keep)
 
     def kappa_from(o, wet):
         gate = jax.nn.sigmoid(o + b_head[0])
@@ -469,20 +473,25 @@
     def add_weights(feats, keep):
         h1_ref, h2_ref, u2_ref, u1_ref, _ = keep
 
-        @pl.loop(0, CHUNKS, unroll=CHUNKS)
-        def _(chunk):
-            bar = jnp.concatenate([obar[chunk, q : q + 1, :] for q in range(8)], axis=1)
-            high, low = halves(u2_ref[chunk] * bar)
-            acc2[...] += dot_nt(h1_ref[chunk], jnp.concatenate([high, low], axis=0))
-            f = jnp.concatenate([feats[chunk, 8 * q : 8 * q + 8, :] for q in range(8)], axis=1)
-            f = f * bar
+        for first in range(0, CHUNKS, 2):
+            pair_of = (first, first + 1)
+            bars = [
+                jnp.concatenate([obar[c, q : q + 1, :] for q in range(8)], axis=1) for c in pair_of
+            ]
+            split = [halves(u2_ref[c] * bar) for c, bar in zip(pair_of, bars)]
+            beside = [jnp.concatenate(x, axis=0) for x in split]
+            h1 = jnp.concatenate([h1_ref[c] for c in pair_of], axis=1)
+            acc2[...] += dot_nt(h1, jnp.concatenate(beside, axis=1))
+            f = [feats[c, 8 * q : 8 * q + 8, :] for c in pair_of for q in range(8)]
+            f = jnp.concatenate(f, axis=1) * jnp.concatenate(bars, axis=1)
             high = f.astype(BF16).astype(F32)
             stacked = jnp.concatenate([high, f - high], axis=0).astype(BF16)
-            acc1[...] += dot_nt(stacked, u1_ref[chunk])
-            weighted = h2_ref[chunk] * bar
-            heads = weighted[:, :COLS]
+            acc1[...] += dot_nt(stacked, jnp.concatenate([u1_ref[c] for c in pair_of], axis=1))
+            weighted = [h2_ref[c] * bar for c, bar in zip(pair_of, bars)]
+            heads = weighted[0][:, :COLS] + weighted[1][:, :COLS]
             for q in range(1, 8):
-                heads = heads + weighted[:, COLS * q : COLS * (q + 1)]
+                lanes = slice(COLS * q, COLS * (q + 1))
+                heads = heads + (weighted[0][:, lanes] + weighted[1][:, lanes])
             acch[...] += heads
 
     def pull_state(by_feat, store):

time: 47.9 us -> 44.3 us (0.925)
  Pallas kernels: 46.5 us -> 42.9 us
    pallas_call x1, Pallas kernels: 45.8 us -> 42.2 us  [per_device(): run(tracers.reshape(field), land_mask, level_counts, fold_partner.reshape...]
where the time goes in v8:
time: 44.3 us; the launch traced here: 44.2 us
  Pallas kernels  42.9 us (97%)
  between operations  1.29 us (3%)
    pallas_call x1, Pallas kernels, per_device(): run(tracers.reshape(field), land_mask, level_counts, fold_partner.reshape...  42.2 us

profile of v8, /device:TPU:1, one launch (start us, length us, event | category | flops | bytes accessed | tf_op | source)
XLA Modules:
  0.0 44.2 jit_solution(2515184159548257171)
XLA Ops:
  1.3 42.2 %adjoint_steps.1 = (f32[8,16,128]{2,1,0:T(8,128)S(1)}, f32[8,16,128]{2,1,0:T(8,128)S(1)}, f32[6,128]{1,0:T(8,128)S(1)}, f32[128,128]{1,0:T(8,128)S(1)}, f32[1,128]{1,0:T(1,128)S(1)}) custom-call(f32[8,16,128]{2,1,0:T(8,128)} %bitcast.9, s32[16,128]{1,0:T(8,128)} %refs_1_.1, s32[16,128]{1,0:T(8,128)} %refs_2_.1, s32[1,128]{1,0:T(1,128)} %bitcast.11, ...), custom_call_target="tpu_custom_call" | custom-call | tf_op jit(solution)/shard_map/adjoint_steps/pallas_call | solution.py:775
  43.5 0.7 %hand_over.1 = (f32[8,16,128]{2,1,0:T(8,128)}, f32[8,16,128]{2,1,0:T(8,128)}, f32[6,128]{1,0:T(8,128)}, f32[128,128]{1,0:T(8,128)}, f32[1,128]{1,0:T(1,128)}) custom-call(f32[8,16,128]{2,1,0:T(8,128)S(1)} %get-tuple-element.15.refs_0_, f32[8,16,128]{2,1,0:T(8,128)S(1)} %get-tuple-element.16.refs_1_, f32[6,128]{1,0:T(8,128)S(1)} %get-tuple-element.17.refs_2_, ...), custom_call_target="tpu_custom_call" | custom-call | tf_op jit(solution)/shard_map/hand_over/pallas_call | solution.py:780
